TPU v7x, 512 devices: a whole 4x4x16 slice. The times are simulated.
512 devices in a mesh: img: 64 (over y, z_lo, x), tpl: 4 (over z_hi), pix: 2 (over core).
Axes of the slice: x: 4, y: 4, z: 16 (z_hi: 4, z_lo: 4; z = z_hi * 4 + z_lo), core: 2. Of those that a mesh axis runs over, the one named last changes fastest.
Arguments:
- images: bfloat16 [16384, 128, 128], P(('img', 'tpl'), 'pix'), may hold values from -6 to 6
- conformers: float32 [8, 3, 4096], replicated, may hold values from -96 to 96
- atom_types: int32 [4096], replicated, may hold values from 0 to 4
- type_amp: float32 [5], replicated, may hold values from 0.3 to 3
- type_width: float32 [5], replicated, may hold values from 0.8 to 2.5
- view_angles: float32 [256, 3], replicated, may hold values from -3.140625 to 3.140625
- template_conf: int32 [512], P(('tpl', 'img')), may hold values from 0 to 7
- template_view: int32 [512], P(('tpl', 'img')), may hold values from 0 to 255
- group_ids: int32 [16384], P('img'), may hold values from 0 to 255
- group_prec: float32 [256], replicated, may hold values from 0.3 to 45
Outputs:
- averages: float32 [512, 128, 128], P(('tpl', 'img'), 'pix')
- loglik: float32 [16384], P(('img', 'tpl'))
All inputs are finite; a program needn't handle non-finite values.
Results may differ from a plain program's by a relative error of at most 0.013.
Values may be sent and summed in bfloat16 or wider, within the bound.
A program may use at most 64 MiB of HBM per device.

v0:
```python
import jax
import jax.numpy as jnp
from jax import lax
from jax.sharding import PartitionSpec as P


def atom_tables(atom_types, type_amp, type_width):
    hits = atom_types[:, None] == jnp.arange(type_amp.shape[0], dtype=jnp.int32)[None, :]
    atom_amp = jnp.sum(jnp.where(hits, type_amp[None, :], 0.0), axis=1) * 0.0625
    widths = jnp.sum(jnp.where(hits, type_width[None, :], 0.0), axis=1)
    return (atom_amp, 0.5 / (widths * widths))


def view_rows(angles):
    cos_phi = jnp.cos(angles[0])
    sin_phi = jnp.sin(angles[0])
    cos_theta = jnp.cos(angles[1])
    sin_theta = jnp.sin(angles[1])
    cos_psi = jnp.cos(angles[2])
    sin_psi = jnp.sin(angles[2])
    first_row = (
        cos_phi * cos_theta * cos_psi - sin_phi * sin_psi,
        -cos_phi * cos_theta * sin_psi - sin_phi * cos_psi,
        cos_phi * sin_theta,
    )
    second_row = (
        sin_phi * cos_theta * cos_psi + cos_phi * sin_psi,
        -sin_phi * cos_theta * sin_psi + cos_phi * cos_psi,
        sin_phi * sin_theta,
    )
    return (first_row, second_row)


def render_one(coords, angles, atom_amp, inv_spread, row_pos, col_pos):
    first_row, second_row = view_rows(angles)
    across = first_row[0] * coords[0] + first_row[1] * coords[1] + first_row[2] * coords[2]
    down = second_row[0] * coords[0] + second_row[1] * coords[1] + second_row[2] * coords[2]
    col_table = jnp.exp(-jnp.square(col_pos[None, :] - across[:, None]) * inv_spread[:, None])
    row_table = atom_amp[:, None] * jnp.exp(
        -jnp.square(row_pos[None, :] - down[:, None]) * inv_spread[:, None]
    )
    return lax.dot_general(
        row_table,
        col_table,
        (((0,), (0,)), ((), ())),
        precision=lax.Precision.HIGHEST,
        preferred_element_type=jnp.float32,
    )


def group_lookup(group_ids, group_prec):
    hits = group_ids[:, None] == jnp.arange(group_prec.shape[0], dtype=jnp.int32)[None, :]
    return jnp.sum(jnp.where(hits, group_prec[None, :], 0.0), axis=1)


def on_device(
    images,
    conformers,
    atom_types,
    type_amp,
    type_width,
    view_angles,
    template_conf,
    template_view,
    group_ids,
    group_prec,
):
    img_dev, half_rows, side = images.shape
    pixel_count = half_rows * side
    flat_rows = images.reshape(img_dev, pixel_count)
    pix_index = lax.axis_index("pix")
    tpl_index = lax.axis_index("tpl")
    tpl_count = lax.axis_size("tpl")
    atom_amp, inv_spread = atom_tables(atom_types, type_amp, type_width)
    col_pos = jnp.arange(side).astype(jnp.float32) - side * 0.5 + 0.5
    row_pos = (
        (pix_index * half_rows + jnp.arange(half_rows, dtype=jnp.int32)).astype(jnp.float32)
        - side * 0.5
        + 0.5
    )
    own_coords = jnp.take(conformers, template_conf, axis=0)
    own_angles = jnp.take(view_angles, template_view, axis=0)
    own_rendered = jax.vmap(
        lambda coords, angles: render_one(coords, angles, atom_amp, inv_spread, row_pos, col_pos)
    )(own_coords, own_angles)
    rendered_count = own_rendered.shape[0]
    own_rendered = own_rendered.astype(jnp.bfloat16).reshape(rendered_count, pixel_count)
    templates = lax.all_gather(own_rendered, "img", axis=0, tiled=True)
    tpl_dev = templates.shape[0]
    part_norms = jnp.sum(jnp.square(templates.astype(jnp.float32)), axis=1)
    precision_rows = group_lookup(group_ids, group_prec)
    img_grp = precision_rows.shape[0]
    group_images = lax.all_gather(flat_rows, "tpl", axis=0, tiled=True)
    part_scores = lax.dot_general(
        group_images, templates, (((1,), (1,)), ((), ())), preferred_element_type=jnp.float32
    )
    anchor = jnp.zeros((), jnp.int32)
    score_block = lax.dynamic_update_slice(
        jnp.zeros((img_grp, tpl_dev * tpl_count), jnp.float32),
        part_scores,
        (anchor, tpl_index * tpl_dev),
    )
    norm_block = lax.dynamic_update_slice(
        jnp.zeros((tpl_dev * tpl_count,), jnp.float32), part_norms, (tpl_index * tpl_dev,)
    )
    full_scores, full_norms = lax.psum((score_block, norm_block), ("tpl", "pix"))
    logits = precision_rows[:, None] * full_scores * lax.rsqrt(full_norms + 1e-06)[None, :]
    maximum = jnp.max(logits, axis=1)
    weights = jnp.exp(logits - maximum[:, None])
    totals = jnp.sum(weights, axis=1)
    own_weights = lax.dynamic_slice_in_dim(weights, tpl_index * tpl_dev, tpl_dev, 1)
    resp = (own_weights / totals[:, None]).astype(jnp.bfloat16)
    loglik = maximum + jnp.log(totals)
    own_loglik = lax.dynamic_slice_in_dim(loglik, tpl_index * img_dev, img_dev, 0)
    own_sums = lax.psum_scatter(
        lax.dot_general(
            resp, group_images, (((0,), (0,)), ((), ())), preferred_element_type=jnp.float32
        ),
        "img",
        scatter_dimension=0,
        tiled=True,
    )
    part_squares = jnp.sum(jnp.square(own_sums), axis=1)
    full_squares = lax.psum(part_squares, "pix")
    scale = lax.rsqrt(full_squares / (side * side) + 1e-06)
    averages = (own_sums * scale[:, None]).reshape(rendered_count, half_rows, side)
    return (averages, own_loglik)


def solution(mesh):
    placed = (
        P(("img", "tpl"), "pix", None),
        P(),
        P(),
        P(),
        P(),
        P(),
        P(("tpl", "img")),
        P(("tpl", "img")),
        P("img"),
        P(),
    )
    return jax.shard_map(
        on_device,
        mesh=mesh,
        in_specs=placed,
        out_specs=(P(("tpl", "img"), "pix", None), P(("img", "tpl"))),
        check_vma=False,
    )
```

profile of v0, /device:TPU:1, one launch (start us, length us, event | category | flops | bytes accessed | tf_op | source)
XLA Modules:
  0.0 1392.9 jit_solution(15018643670695546310)
XLA Ops:
  7.2 0.0 copy-start
  7.2 0.0 all-gather.6.cloned.1.call-start
  7.2 0.7 compare_select_fusion
  7.9 0.7 compare_and_fusion
  8.6 0.8 copy.15
  9.5 0.6 gather_fusion
  10.0 0.1 broadcast_select_fusion.1
  10.1 0.3 add_reduce_fusion.1
  10.4 0.0 copy-done
  10.4 0.9 gather_fusion.1
  11.4 0.1 broadcast_select_fusion
  11.5 0.9 select_reduce_fusion.2
  12.4 0.1 multiply_add_fusion.1
  12.5 0.0 copy-start.2
  12.5 4.2 fusion.16
  16.7 0.6 reshape.202
  17.4 0.0 all-gather.6.cloned.1.call-update
  17.4 0.0 all-gather.4.cloned.1.call-start
  17.4 0.0 copy-done.2
  17.4 1.7 copy.20
  19.2 0.0 all-gather.4.cloned.1.call-update
  19.2 0.0 all-reduce.4.cloned.1.call-start
  19.2 314.0 %all-gather.6.cloned.1.call-done = bf16[64,2,8192]{2,1,0:T(2,128)(2,1)} async-done(((bf16[1,2,8192]{2,1,0:T(2,128)(2,1)}), bf16[64,2,8192]{2,1,0:T(2,128)(2,1)}) %all-gather.6.cloned.1.call-update) | async-done | bytes 2097168 | tf_op jit(solution)/shard_map/all_gather | solution.py:88
  333.2 2.7 reshape.203
  336.0 0.0 copy-start.3
  336.0 0.0 copy-start.4
  336.0 204.9 %all-gather.4.cloned.1.call-done = bf16[256,8192]{1,0:T(8,128)(2,1)} async-done(((bf16[64,8192]{1,0:T(8,128)(2,1)}), bf16[256,8192]{1,0:T(8,128)(2,1)}) %all-gather.4.cloned.1.call-update) | async-done | bytes 4194320 | tf_op jit(solution)/shard_map/all_gather | solution.py:93
  540.9 3.7 fusion.15
  544.6 0.0 copy-start.1
  544.7 0.8 copy-done.1
  545.5 0.0 all-reduce.4.cloned.1.call-update
  545.5 0.0 all-reduce.6.cloned.1.call-start
  545.5 0.0 copy-done.3
  545.5 0.0 copy-done.4
  545.6 0.2 select_reduce_fusion
  545.7 0.5 multiply_reduce_fusion
  546.2 0.2 dynamic_update_slice.7
  546.5 18.4 %psum.22 = f32[512]{0:T(512)S(1)} all-reduce(f32[512]{0:T(512)S(1)} %dynamic_update_slice.7), channel_id=1, replica_groups=mesh['img'=64,'tpl'=4,'pix'=2] {'tpl','pix'}, use_global_device_ids=true, to_apply=%region_5.6 | all-reduce | flops 512 | bytes 4096 | tf_op jit(solution)/shard_map/psum | solution.py:106
  564.8 77.6 %all-reduce.4.cloned.1.call-done = f32[256,512]{0,1:T(8,128)} async-done(((f32[256,512]{0,1:T(8,128)}), f32[256,512]{0,1:T(8,128)}) %all-reduce.4.cloned.1.call-update) | async-done | bytes 524304 | tf_op jit(solution)/shard_map/psum | solution.py:106
  642.5 1.2 fusion.25
  643.6 1.2 fusion.29
  644.9 4.9 fusion.26
  649.7 0.0 all-reduce.6.cloned.1.call-update
  649.8 1.3 dynamic-slice
  651.7 683.5 %all-reduce.6.cloned.1.call-done = f32[128,8192]{1,0:T(8,128)} async-done(((f32[128,8192]{1,0:T(8,128)}), f32[128,8192]{1,0:T(8,128)}) %all-reduce.6.cloned.1.call-update) | async-done | bytes 4194320
  1335.2 1.1 multiply_reduce_fusion.1
  1336.4 0.6 dynamic_slice.7
  1336.9 47.7 %psum.23 = f32[2]{0:T(128)S(1)} all-reduce(f32[2]{0:T(128)S(1)} %multiply_reduce_fusion.1), channel_id=1, replica_groups=mesh['img'=64,'tpl'=4,'pix'=2] {'pix'}, use_global_device_ids=true, to_apply=%region_10.11 | all-reduce | flops 2 | bytes 16 | tf_op jit(solution)/shard_map/psum | solution.py:124
  1384.7 1.0 multiply_bitcast_fusion
  1385.7 0.6 copy.21
  (10 shorter events, 0.1 us)
Async XLA Ops:
  7.2 3.3 copy-start
  7.2 326.1 %all-gather.6.cloned.1.call-start = ((), (), s32[]{:S(2)}) async-start(), calls=%async_computation.2 | async-start | bytes 2129920 | tf_op jit(solution)/shard_map/all_gather | solution.py:88
  12.5 4.9 copy-start.2
  17.4 523.5 %all-gather.4.cloned.1.call-start = ((), (), s32[]{:S(2)}) async-start(), calls=%async_computation | async-start | bytes 5242880 | tf_op jit(solution)/shard_map/all_gather | solution.py:93
  19.2 623.3 %all-reduce.4.cloned.1.call-start = ((), (), s32[]{:S(2)}) async-start(), calls=%async_computation.1 | async-start | bytes 1048576 | tf_op jit(solution)/shard_map/psum | solution.py:106
  336.0 209.6 %copy-start.3 = (f32[256]{0:T(256)S(1)}, f32[256]{0:T(256)}, u32[]{:S(2)}) copy-start(f32[256]{0:T(256)} %param.19) | copy-start | bytes 3076
  336.0 209.6 %copy-start.4 = (s32[256]{0:T(256)S(1)}, s32[256]{0:T(256)}, u32[]{:S(2)}) copy-start(s32[256]{0:T(256)} %param.18) | copy-start | bytes 3076
  544.6 0.8 copy-start.1
  545.5 789.7 %all-reduce.6.cloned.1.call-start = ((), (), s32[]{:S(2)}) async-start(), calls=%async_computation.3 | async-start | bytes 8388608
Sparse Core Ops, SparseCore 0:
  17.5 315.6 all-gather.5
  335.3 205.4 all-gather.3
  545.6 96.7 all-reduce.3
  649.9 685.2 all-reduce.5
where the time goes:
time: 1390 us
  waiting for transfers between devices  1280 us (92%)
  blocking collectives  66.1 us (5%)
  between operations  14.6 us (1%)
    unnamed x5, waiting for transfers between devices  684 us
    all_gather x1, waiting for transfers between devices, on_device(): templates = lax.all_gather(own_rendered, 'img', axis=0, tiled=True)  314 us
    all_gather x1, waiting for transfers between devices, on_device(): group_images = lax.all_gather(flat_rows, 'tpl', axis=0, tiled=True)  205 us
    psum x1, waiting for transfers between devices, on_device(): lax.psum((score_block, norm_block), ('tpl', 'pix'))  77.6 us
    psum x1, blocking collectives, on_device(): full_squares = lax.psum(part_squares, 'pix')  47.7 us
  transfers between devices with their start and end apart: 4, of which 4 were waited for; matrix products, arithmetic and copies ran while one was open for 0% of the time, Pallas kernels for 0%

commit v1 on v0

v1 whole, which is shorter than its diff:
```python
import functools

import jax
import jax.numpy as jnp
from jax import lax
from jax.experimental import pallas as pl
from jax.experimental.pallas import tpu as pltpu
from jax.sharding import PartitionSpec as P

NX, NY, NZL = 4, 4, 4
MESH = pl.DeviceIdType.MESH
NT = (((1,), (1,)), ((), ()))


def view_rows(angles):
    cos_phi = jnp.cos(angles[0])
    sin_phi = jnp.sin(angles[0])
    cos_theta = jnp.cos(angles[1])
    sin_theta = jnp.sin(angles[1])
    cos_psi = jnp.cos(angles[2])
    sin_psi = jnp.sin(angles[2])
    return (
        cos_phi * cos_theta * cos_psi - sin_phi * sin_psi,
        -cos_phi * cos_theta * sin_psi - sin_phi * cos_psi,
        cos_phi * sin_theta,
        sin_phi * cos_theta * cos_psi + cos_phi * sin_psi,
        -sin_phi * cos_theta * sin_psi + cos_phi * cos_psi,
        sin_phi * sin_theta,
    )


def group_lookup(group_ids, group_prec):
    hits = group_ids[:, None] == jnp.arange(group_prec.shape[0], dtype=jnp.int32)[None, :]
    return jnp.sum(jnp.where(hits, group_prec[None, :], 0.0), axis=1)


def em_kernel(
    side,
    kc,
    rows_sm,
    conf_sm,
    tamp_sm,
    twid_sm,
    images,
    conformers,
    types,
    prec,
    out,
    loglik,
    img_buf,
    tsend,
    tbuf,
    tall,
    ssend,
    srecv,
    lsend,
    lrecv,
    rall,
    sums,
    rsf_send,
    rsf_recv,
    rsb_send,
    rsb_recv,
    fsend,
    fin,
    stage,
    orecv,
    acc,
    i_s,
    i_r,
    x_s,
    x_r,
    t_s,
    t_r,
    af_s,
    af_r,
    ab_s,
    ab_r,
    s_s,
    s_r,
    l_s,
    l_r,
    r_s,
    r_r,
    rf_s,
    rf_r,
    rb_s,
    rb_r,
    f_s,
    f_r,
    o_s,
    o_r,
    own_sem,
):
    plane = NX * NY
    img = lax.axis_index("img")
    tpl = lax.axis_index("tpl")
    pix = lax.axis_index("pix")
    nz = NZL * lax.axis_size("tpl")
    x = lax.rem(img, NX)
    zl = lax.rem(lax.div(img, NX), NZL)
    y = lax.div(img, NX * NZL)
    z = tpl * NZL + zl
    me = y * NX + x
    half_rows = side // 2
    part_rows = half_rows // plane
    part = part_rows * side
    tile_rows = 2 * part_rows
    nimg = images.shape[0]
    fwd = nz // 2
    bwd = nz - 1 - fwd

    def mate(q):
        qy = lax.div(q, NX)
        qx = lax.rem(q, NX)
        return ((qy * NZL + zl) * NX + qx, tpl, pix)

    def along(step):
        zz = lax.rem(z + step + nz, nz)
        zt = lax.div(zz, NZL)
        zr = lax.rem(zz, NZL)
        return ((y * NZL + zr) * NX + x, zt, pix)

    up, down = along(1), along(-1)
    twin = (img, tpl, 1 - pix)

    def other(d):
        return lax.rem(me + d, plane)

    def rows_of(q):
        return pl.ds(pl.multiple_of(q * tile_rows, tile_rows), tile_rows)

    def remote(src, dst, ss, rs, dev):
        return pltpu.make_async_remote_copy(
            src_ref=src, dst_ref=dst, send_sem=ss, recv_sem=rs, device_id=dev, device_id_type=MESH
        )

    def each(body):
        @pl.loop(1, plane)
        def _(d):
            body(other(d))

    bar = pltpu.get_barrier_semaphore()
    each(lambda q: pl.semaphore_signal(bar, inc=1, device_id=mate(q), device_id_type=MESH))
    for dev in (up, down, twin):
        pl.semaphore_signal(bar, inc=1, device_id=dev, device_id_type=MESH)
    pl.semaphore_wait(bar, plane - 1 + 3)

    def image_copy(q, src_of):
        cols = pl.ds(pl.multiple_of(q * part, part), part)
        return remote(
            images.at[:, cols], img_buf.at[pix, src_of], i_s.at[q], i_r.at[src_of], mate(q)
        )

    each(lambda q: image_copy(q, me).start())
    own = pltpu.make_async_copy(
        images.at[:, pl.ds(pl.multiple_of(me * part, part), part)], img_buf.at[pix, me], own_sem
    )
    own.start()

    conf = conf_sm[pix]
    s_idx = lax.broadcasted_iota(jnp.int32, (side, 1), 0)
    owner = s_idx // tile_rows
    in_tile = lax.rem(s_idx, tile_rows)
    row_id = (in_tile // part_rows) * half_rows + owner * part_rows + lax.rem(in_tile, part_rows)
    row_pos = row_id.astype(jnp.float32) - side * 0.5 + 0.5
    col_pos = s_idx.astype(jnp.float32) - side * 0.5 + 0.5
    acc[...] = jnp.zeros_like(acc)

    @pl.loop(0, types.shape[1] // kc)
    def _(k):
        sl = pl.ds(pl.multiple_of(k * kc, kc), kc)
        kind = types[:, sl]
        amp = jnp.zeros((1, kc), jnp.float32)
        width = jnp.zeros((1, kc), jnp.float32)
        for j in range(tamp_sm.shape[0]):
            amp = jnp.where(kind == j, tamp_sm[j], amp)
            width = jnp.where(kind == j, twid_sm[j], width)
        amp = amp * 0.0625
        spread = 0.5 / (width * width)
        c0 = conformers[conf, 0:1, sl]
        c1 = conformers[conf, 1:2, sl]
        c2 = conformers[conf, 2:3, sl]
        across = rows_sm[0] * c0 + rows_sm[1] * c1 + rows_sm[2] * c2
        below = rows_sm[3] * c0 + rows_sm[4] * c1 + rows_sm[5] * c2
        dc = col_pos - across
        dr = row_pos - below
        col = jnp.exp(-(dc * dc) * spread)
        row = amp * jnp.exp(-(dr * dr) * spread)
        col_hi = col.astype(jnp.bfloat16)
        col_lo = (col - col_hi.astype(jnp.float32)).astype(jnp.bfloat16)
        row_hi = row.astype(jnp.bfloat16)
        row_lo = (row - row_hi.astype(jnp.float32)).astype(jnp.bfloat16)
        total = lax.dot_general(row_hi, col_lo, NT, preferred_element_type=jnp.float32)
        total += lax.dot_general(row_lo, col_hi, NT, preferred_element_type=jnp.float32)
        total += lax.dot_general(row_hi, col_hi, NT, preferred_element_type=jnp.float32)
        acc[...] += total

    tsend[...] = acc[...].astype(jnp.bfloat16).astype(jnp.float32)

    def template_copy(q, src_of):
        return remote(tsend.at[rows_of(q)], tbuf.at[rows_of(src_of)], t_s.at[q], t_r.at[src_of], mate(q))

    each(lambda q: template_copy(q, me).start())
    tbuf[rows_of(me), :] = tsend[rows_of(me), :]
    each(lambda q: template_copy(q, q).wait_recv())
    for k in range(tile_rows):
        tall[z, :, k * side : (k + 1) * side] = tbuf[pl.ds(k, plane, stride=tile_rows), :].astype(
            jnp.bfloat16
        )

    def up_block(s, first):
        b = lax.rem(first - s + 2 * nz, nz)
        return remote(tall.at[b], tall.at[b], af_s.at[s], af_r.at[s], up)

    def down_block(s, first):
        b = lax.rem(first + s, nz)
        return remote(tall.at[b], tall.at[b], ab_s.at[s], ab_r.at[s], down)

    swap = remote(img_buf.at[pix], img_buf.at[pix], x_s, x_r, twin)
    for s in range(fwd):
        if s > 0:
            up_block(s - 1, z - 1).wait_recv()
        up_block(s, z).start()
        if s < bwd:
            if s > 0:
                down_block(s - 1, z + 1).wait_recv()
            down_block(s, z).start()
        if s == min(2, fwd - 1):
            own.wait()
            each(lambda q: image_copy(q, q).wait_recv())
            swap.start()
    up_block(fwd - 1, z - 1).wait_recv()
    if bwd > 0:
        down_block(bwd - 1, z + 1).wait_recv()
    remote(img_buf.at[1 - pix], img_buf.at[1 - pix], x_s, x_r, twin).wait_recv()

    ntpl = nz * plane
    both = tall[...].reshape(ntpl, 2 * part)
    tf = both.astype(jnp.float32)
    sq = tf * tf
    sq_hi = sq.astype(jnp.bfloat16)
    sq_lo = (sq - sq_hi.astype(jnp.float32)).astype(jnp.bfloat16)
    ones = jnp.ones((8, 2 * part), jnp.bfloat16)
    norm = lax.dot_general(ones, sq_hi, NT, preferred_element_type=jnp.float32)
    norm += lax.dot_general(ones, sq_lo, NT, preferred_element_type=jnp.float32)

    def score_copy(q, src_of):
        return remote(ssend.at[q], srecv.at[src_of], s_s.at[q], s_r.at[src_of], mate(q))

    group = 4

    @pl.loop(0, plane // group)
    def _(g):
        at = pl.ds(g * group, group)
        lhs = img_buf[0, at].reshape(group * nimg, part)
        res = lax.dot_general(lhs, tall[:, :, :part].reshape(ntpl, part), NT, preferred_element_type=jnp.float32)
        lhs = img_buf[1, at].reshape(group * nimg, part)
        res += lax.dot_general(lhs, tall[:, :, part:].reshape(ntpl, part), NT, preferred_element_type=jnp.float32)
        ssend[at, :nimg, :] = res.reshape(group, nimg, ntpl)
        ssend[at, nimg:, :] = jnp.broadcast_to(norm[None], (group, 8, ntpl))

    each(lambda q: score_copy(q, me).start())
    each(lambda q: score_copy(q, q).wait_recv())
    srecv[pl.ds(me, 1)] = ssend[pl.ds(me, 1)]
    full = jnp.sum(srecv[...], axis=0)
    logits = prec[...] * full[:nimg] * lax.rsqrt(full[nimg : nimg + 1] + 1e-06)
    lsend[...] = logits
    logit_copy = remote(lsend, lrecv, l_s, l_r, twin)
    logit_copy.start()
    logit_copy.wait_recv()
    theirs = lrecv[...]
    top = jnp.maximum(
        jnp.max(logits, axis=1, keepdims=True), jnp.max(theirs, axis=1, keepdims=True)
    )
    weights = jnp.exp(logits - top)
    totals = jnp.sum(weights, axis=1, keepdims=True) + jnp.sum(
        jnp.exp(theirs - top), axis=1, keepdims=True
    )
    loglik[...] = top + jnp.log(totals)
    rall[pl.ds(me, 1)] = (weights / totals).astype(jnp.bfloat16)[None]

    def resp_copy(q, src_of):
        return remote(rall.at[src_of], rall.at[src_of], r_s.at[q], r_r.at[src_of], mate(q))

    each(lambda q: resp_copy(q, me).start())
    each(lambda q: resp_copy(q, q).wait_recv())

    resp = rall[...].reshape(plane * nimg, ntpl).astype(jnp.float32).T.astype(jnp.bfloat16)
    for h in range(2):
        res = lax.dot_general(
            resp,
            img_buf[h].reshape(plane * nimg, part),
            (((1,), (0,)), ((), ())),
            preferred_element_type=jnp.float32,
        )
        sums[:, :, h * part : (h + 1) * part] = res.reshape(nz, plane, part)

    for s in range(fwd):
        val = sums[lax.rem(z + fwd - s, nz)]
        if s > 0:
            remote(rsf_send.at[s - 1], rsf_recv.at[s - 1], rf_s.at[s - 1], rf_r.at[s - 1], up).wait_recv()
            val = val + rsf_recv[s - 1].astype(jnp.float32)
        rsf_send[s] = val.astype(jnp.bfloat16)
        remote(rsf_send.at[s], rsf_recv.at[s], rf_s.at[s], rf_r.at[s], up).start()
        if s < bwd:
            val = sums[lax.rem(z - bwd + s + nz, nz)]
            if s > 0:
                remote(rsb_send.at[s - 1], rsb_recv.at[s - 1], rb_s.at[s - 1], rb_r.at[s - 1], down).wait_recv()
                val = val + rsb_recv[s - 1].astype(jnp.float32)
            rsb_send[s] = val.astype(jnp.bfloat16)
            remote(rsb_send.at[s], rsb_recv.at[s], rb_s.at[s], rb_r.at[s], down).start()
    val = sums[z]
    remote(rsf_send.at[fwd - 1], rsf_recv.at[fwd - 1], rf_s.at[fwd - 1], rf_r.at[fwd - 1], up).wait_recv()
    val = val + rsf_recv[fwd - 1].astype(jnp.float32)
    if bwd > 0:
        remote(rsb_send.at[bwd - 1], rsb_recv.at[bwd - 1], rb_s.at[bwd - 1], rb_r.at[bwd - 1], down).wait_recv()
        val = val + rsb_recv[bwd - 1].astype(jnp.float32)
    for k in range(tile_rows):
        fsend[pl.ds(k, plane, stride=tile_rows), :] = val[:, k * side : (k + 1) * side]

    def final_copy(q, src_of):
        return remote(fsend.at[rows_of(q)], fin.at[rows_of(src_of)], f_s.at[q], f_r.at[src_of], mate(q))

    each(lambda q: final_copy(q, me).start())
    fin[rows_of(me), :] = fsend[rows_of(me), :]
    each(lambda q: final_copy(q, q).wait_recv())
    whole = fin[...]
    squares = jnp.sum(jnp.sum(whole * whole, axis=1, keepdims=True), axis=0, keepdims=True)
    scaled = whole * lax.rsqrt(squares / (side * side) + 1e-06)
    for q in range(plane):
        for h in range(2):
            at = q * tile_rows + h * part_rows
            stage[h, q * part_rows : (q + 1) * part_rows, :] = scaled[at : at + part_rows, :]
    half_copy = remote(stage.at[1 - pix], orecv, o_s, o_r, twin)
    half_copy.start()
    out[pl.ds(pix, 1)] = stage[pl.ds(pix, 1)]
    half_copy.wait_recv()
    out[pl.ds(1 - pix, 1)] = orecv[...][None]

    each(lambda q: image_copy(q, me).wait_send())
    each(lambda q: template_copy(q, me).wait_send())
    each(lambda q: score_copy(q, me).wait_send())
    each(lambda q: resp_copy(q, me).wait_send())
    each(lambda q: final_copy(q, me).wait_send())
    swap.wait_send()
    logit_copy.wait_send()
    half_copy.wait_send()
    for s in range(fwd):
        up_block(s, z).wait_send()
        remote(rsf_send.at[s], rsf_recv.at[s], rf_s.at[s], rf_r.at[s], up).wait_send()
    for s in range(bwd):
        down_block(s, z).wait_send()
        remote(rsb_send.at[s], rsb_recv.at[s], rb_s.at[s], rb_r.at[s], down).wait_send()


def on_device(
    images,
    conformers,
    atom_types,
    type_amp,
    type_width,
    view_angles,
    template_conf,
    template_view,
    group_ids,
    group_prec,
):
    nimg, half_rows, side = images.shape
    plane = NX * NY
    nz = NZL * lax.axis_size("tpl")
    part = half_rows * side // plane
    ntpl = nz * plane
    fwd = nz // 2
    bwd = max(nz - 1 - fwd, 1)
    flat = images.reshape(nimg, half_rows * side)
    pix = lax.axis_index("pix")
    angles = jnp.take(view_angles, lax.dynamic_index_in_dim(template_view, pix, keepdims=False), axis=0)
    rows = jnp.stack(view_rows(angles))
    own_ids = lax.dynamic_slice_in_dim(group_ids, lax.axis_index("tpl") * nimg, nimg)
    prec = group_lookup(own_ids, group_prec)[:, None]
    bf16, f32 = jnp.bfloat16, jnp.float32
    vmem = pl.BlockSpec(memory_space=pltpu.VMEM)
    smem = pl.BlockSpec(memory_space=pltpu.SMEM)
    dma = pltpu.SemaphoreType.DMA
    natoms = atom_types.shape[0]
    averages, loglik = pl.pallas_call(
        functools.partial(em_kernel, side, min(512, natoms)),
        out_shape=(
            jax.ShapeDtypeStruct((2, half_rows, side), f32),
            jax.ShapeDtypeStruct((nimg, 1), f32),
        ),
        in_specs=[smem] * 4 + [vmem] * 4,
        out_specs=(vmem, vmem),
        scratch_shapes=[
            pltpu.VMEM((2, plane, nimg, part), bf16),
            pltpu.VMEM((side, side), f32),
            pltpu.VMEM((side, side), f32),
            pltpu.VMEM((nz, plane, 2 * part), bf16),
            pltpu.VMEM((plane, nimg + 8, ntpl), f32),
            pltpu.VMEM((plane, nimg + 8, ntpl), f32),
            pltpu.VMEM((nimg, ntpl), f32),
            pltpu.VMEM((nimg, ntpl), f32),
            pltpu.VMEM((plane, nimg, ntpl), bf16),
            pltpu.VMEM((nz, plane, 2 * part), f32),
            pltpu.VMEM((fwd, plane, 2 * part), bf16),
            pltpu.VMEM((fwd, plane, 2 * part), bf16),
            pltpu.VMEM((bwd, plane, 2 * part), bf16),
            pltpu.VMEM((bwd, plane, 2 * part), bf16),
            pltpu.VMEM((side, side), f32),
            pltpu.VMEM((side, side), f32),
            pltpu.VMEM((2, half_rows, side), f32),
            pltpu.VMEM((half_rows, side), f32),
            pltpu.VMEM((side, side), f32),
            dma((plane,)),
            dma((plane,)),
            dma,
            dma,
            dma((plane,)),
            dma((plane,)),
            dma((fwd,)),
            dma((fwd,)),
            dma((bwd,)),
            dma((bwd,)),
            dma((plane,)),
            dma((plane,)),
            dma,
            dma,
            dma((plane,)),
            dma((plane,)),
            dma((fwd,)),
            dma((fwd,)),
            dma((bwd,)),
            dma((bwd,)),
            dma((plane,)),
            dma((plane,)),
            dma,
            dma,
            dma,
        ],
        compiler_params=pltpu.CompilerParams(
            collective_id=0, has_side_effects=True, vmem_limit_bytes=48 * 1024 * 1024
        ),
    )(
        rows,
        template_conf,
        type_amp,
        type_width,
        flat,
        conformers,
        atom_types[None, :],
        prec,
    )
    return averages, loglik[:, 0]


def solution(mesh):
    placed = (
        P(("img", "tpl"), "pix", None),
        P(),
        P(),
        P(),
        P(),
        P(),
        P(("tpl", "img")),
        P(("tpl", "img")),
        P("img"),
        P(),
    )
    return jax.shard_map(
        on_device,
        mesh=mesh,
        in_specs=placed,
        out_specs=(P(("tpl", "img"), "pix", None), P(("img", "tpl"))),
        check_vma=False,
    )
```

time: 1390 us -> 127 us (0.09)
  waiting for transfers between devices: 1280 us -> 0 us
  Pallas kernels: 0 us -> 112 us
  blocking collectives: 66.1 us -> 0 us
    unnamed x5 -> x0, waiting for transfers between devices: 684 us -> none
    all_gather x2 -> x0, waiting for transfers between devices: 519 us -> none  [the longest x1 314 us: on_device(): templates = lax.all_gather(own_rendered, 'img', axis=0, tiled=True)]
    pallas_call x0 -> x1, Pallas kernels: none -> 112 us  [on_device(): pl.pallas_call(functools.partial(em_kernel, side, min(512, natoms)), out_...]
    psum x1 -> x0, waiting for transfers between devices: 77.6 us -> none  [on_device(): lax.psum((score_block, norm_block), ('tpl', 'pix'))]
    psum x2 -> x0, blocking collectives: 66.1 us -> none  [the longest x1 47.7 us: on_device(): full_squares = lax.psum(part_squares, 'pix')]
  transfers between devices with their start and end apart: 4 -> 0, of which waited for: 4 -> 0; matrix products, arithmetic and copies ran while one was open for 0% -> 0% of each run, Pallas kernels for 0% -> 0%
where the time goes in v1:
time: 127 us
  Pallas kernels  112 us (88%)
  between operations  6.93 us (5%)
  local copies, waits for them, and re-layouts  6.08 us (5%)
  other arithmetic  2.24 us (2%)
    pallas_call x1, Pallas kernels, on_device(): pl.pallas_call(functools.partial(em_kernel, side, min(512, natoms)), out_...  112 us
    unnamed x13, local copies, waits for them, and re-layouts  3.26 us

profile of v1, /device:TPU:1, one launch (start us, length us, event | category | flops | bytes accessed | tf_op | source)
XLA Modules:
  0.0 126.9 jit_solution(7358955261398402089)
XLA Ops:
  0.6 0.0 copy-start.4
  0.6 0.8 dynamic_slice.8
  1.5 0.9 select_reduce_fusion
  2.3 1.2 dynamic_slice.7
  5.5 0.8 dynamic-slice_select_fusion
  6.3 0.6 fusion
  11.1 0.1 stack.27.rows_sm
  11.2 0.1 copy.17.prec
  11.3 1.3 %copy.16.conformers = f32[8,3,4096]{2,1,0:T(4,128)S(1)} copy(f32[8,3,4096]{2,0,1:T(8,128)} %param.11) | data formatting | bytes 786432 | tf_op args[1]
  12.6 0.0 copy-done.4
  12.6 0.0 copy-start
  12.6 0.7 copy.20
  13.3 0.0 copy-start.1
  13.3 0.0 copy-start.2
  13.3 0.0 copy-start.3
  13.3 0.0 copy-done
  13.3 0.6 copy-done.1
  14.0 0.0 copy-done.2
  14.0 0.0 copy-done.3
  14.0 111.6 %shard_map.113 = (f32[2,64,128]{2,1,0:T(8,128)S(1)}, f32[64,1]{1,0:T(8,128)S(1)}) custom-call(f32[6]{0:T(128)S(1)} %stack.27.rows_sm, s32[2]{0:T(128)S(1)} %copy-done.1, f32[5]{0:T(128)S(1)} %copy-done.2, f32[5]{0:T(128)S(1)} %copy-done.3, bf16[64,8192]{1,0:T(8,128)(2,1)S(1)} %bitcast.19, f32[8,3,4096]{2,1,0:T(4,128)S(1)} %copy.16.conformers, ...), custom_call_target="tpu_custom_call" | custom-call | tf_op jit(solution)/shard_map/pallas_call | solution.py:387
  125.6 0.6 reduce
  126.2 0.6 copy.22
Async XLA Ops:
  0.6 11.9 %copy-start.4 = (bf16[64,64,128]{2,1,0:T(8,128)(2,1)S(1)}, bf16[64,64,128]{2,1,0:T(8,128)(2,1)}, u32[]{:S(2)}) copy-start(bf16[64,64,128]{2,1,0:T(8,128)(2,1)} %param.10) | copy-start | bytes 3145732
  12.6 0.8 copy-start
  13.3 0.7 copy-start.1
  13.3 0.7 copy-start.2
  13.3 0.7 copy-start.3

commit v2 on v1

v2 whole, which is shorter than its diff:
```python
import functools

import jax
import jax.numpy as jnp
from jax import lax
from jax.experimental import pallas as pl
from jax.experimental.pallas import tpu as pltpu
from jax.sharding import PartitionSpec as P

NX, NY, NZL = 4, 4, 4
MESH = pl.DeviceIdType.MESH
NT = (((1,), (1,)), ((), ()))


EARLY = (0, 1, 2, 3, 4, 12, 14, 15)
LATE = (8, 7, 9, 5, 6, 10, 11, 13)
ORDER = EARLY + LATE
POS = {k: i for i, k in enumerate(ORDER)}
NZ = 16
RELAY = {0: ((1, -1), (15, 1), (2, -2), (14, 2)), 4: ((5, -1), (3, 1), (6, -2)), 12: ((13, -1), (11, 1), (10, 2)), 8: ((9, -1), (7, 1))}
STEPS = (1, -1, 2, -2, 4, -4, 8)


def em_kernel(
    side,
    kc,
    conf_sm,
    view_sm,
    tamp_sm,
    twid_sm,
    images,
    conformers,
    types,
    angles,
    ids,
    group_prec,
    out,
    loglik,
    img_buf,
    tsend,
    tbuf,
    tall,
    ssend,
    srecv,
    lsend,
    lrecv,
    rall,
    own_sums,
    sums,
    rr,
    r2_send,
    r2_recv,
    fsend,
    fin,
    stage,
    orecv,
    acc,
    i_s,
    i_r,
    x_s,
    x_r,
    t_s,
    t_r,
    a_s,
    a_r,
    s_s,
    s_r,
    l_s,
    l_r,
    r_s,
    r_r,
    z_s,
    z_r,
    z2_s,
    z2_r,
    f_s,
    f_r,
    o_s,
    o_r,
    own_sem,
):
    f32, bf16 = jnp.float32, jnp.bfloat16
    plane = NX * NY
    img = lax.axis_index("img")
    tpl = lax.axis_index("tpl")
    pix = lax.axis_index("pix")
    x = lax.rem(img, NX)
    zl = lax.rem(lax.div(img, NX), NZL)
    y = lax.div(img, NX * NZL)
    z = tpl * NZL + zl
    me = y * NX + x
    half_rows = side // 2
    part_rows = half_rows // plane
    part = part_rows * side
    tile_rows = 2 * part_rows
    nimg = images.shape[1]
    half = len(EARLY)
    ntpl = half * plane

    def mate(q):
        qy = lax.div(q, NX)
        qx = lax.rem(q, NX)
        return ((qy * NZL + zl) * NX + qx, tpl, pix)

    def along(step):
        zz = lax.rem(z + step + NZ, NZ)
        zt = lax.div(zz, NZL)
        zr = lax.rem(zz, NZL)
        return ((y * NZL + zr) * NX + x, zt, pix)

    twin = (img, tpl, 1 - pix)

    def rows_of(q):
        return pl.ds(pl.multiple_of(q * tile_rows, tile_rows), tile_rows)

    def remote(src, dst, ss, rs, dev):
        return pltpu.make_async_remote_copy(
            src_ref=src, dst_ref=dst, send_sem=ss, recv_sem=rs, device_id=dev, device_id_type=MESH
        )

    def each(body, first=1, last=plane):
        @pl.loop(first, last)
        def _(d):
            body(lax.rem(me + d, plane))

    bar = pltpu.get_barrier_semaphore()
    each(lambda q: pl.semaphore_signal(bar, inc=1, device_id=mate(q), device_id_type=MESH))
    for step in STEPS:
        pl.semaphore_signal(bar, inc=1, device_id=along(step), device_id_type=MESH)
    pl.semaphore_signal(bar, inc=1, device_id=twin, device_id_type=MESH)

    own = pltpu.make_async_copy(images.at[me], img_buf.at[pix, me], own_sem)
    own.start()

    conf = conf_sm[pix]
    view = angles[pl.ds(view_sm[pix], 1), :]
    cosines = jnp.cos(view)
    sines = jnp.sin(view)
    cos_phi, cos_theta, cos_psi = (cosines[:, i : i + 1] for i in range(3))
    sin_phi, sin_theta, sin_psi = (sines[:, i : i + 1] for i in range(3))
    r00 = cos_phi * cos_theta * cos_psi - sin_phi * sin_psi
    r01 = -cos_phi * cos_theta * sin_psi - sin_phi * cos_psi
    r02 = cos_phi * sin_theta
    r10 = sin_phi * cos_theta * cos_psi + cos_phi * sin_psi
    r11 = -sin_phi * cos_theta * sin_psi + cos_phi * cos_psi
    r12 = sin_phi * sin_theta
    s_idx = lax.broadcasted_iota(jnp.int32, (side, 1), 0)
    owner = s_idx // tile_rows
    in_tile = lax.rem(s_idx, tile_rows)
    row_id = (in_tile // part_rows) * half_rows + owner * part_rows + lax.rem(in_tile, part_rows)
    row_pos = row_id.astype(f32) - side * 0.5 + 0.5
    col_pos = s_idx.astype(f32) - side * 0.5 + 0.5
    acc[...] = jnp.zeros_like(acc)

    @pl.loop(0, types.shape[1] // kc)
    def _(k):
        sl = pl.ds(pl.multiple_of(k * kc, kc), kc)
        kind = types[:, sl]
        amp = jnp.zeros((1, kc), f32)
        width = jnp.zeros((1, kc), f32)
        for j in range(tamp_sm.shape[0]):
            amp = jnp.where(kind == j, tamp_sm[j], amp)
            width = jnp.where(kind == j, twid_sm[j], width)
        amp = amp * 0.0625
        spread = 0.5 / (width * width)
        c0 = conformers[conf, 0:1, sl]
        c1 = conformers[conf, 1:2, sl]
        c2 = conformers[conf, 2:3, sl]
        across = r00 * c0 + r01 * c1 + r02 * c2
        below = r10 * c0 + r11 * c1 + r12 * c2
        dc = col_pos - across
        dr = row_pos - below
        col = jnp.exp(-(dc * dc) * spread)
        row = amp * jnp.exp(-(dr * dr) * spread)
        col_hi = col.astype(bf16)
        col_lo = (col - col_hi.astype(f32)).astype(bf16)
        row_hi = row.astype(bf16)
        row_lo = (row - row_hi.astype(f32)).astype(bf16)
        total = lax.dot_general(row_hi, col_lo, NT, preferred_element_type=f32)
        total += lax.dot_general(row_lo, col_hi, NT, preferred_element_type=f32)
        total += lax.dot_general(row_hi, col_hi, NT, preferred_element_type=f32)
        acc[...] += total

    tsend[...] = acc[...].astype(bf16).astype(f32)

    groups = ids.shape[1]
    at_row = lax.broadcasted_iota(jnp.int32, (nimg, groups), 0)
    at_col = lax.broadcasted_iota(jnp.int32, (nimg, groups), 1)
    own_id = jnp.sum(
        jnp.where(at_col == at_row + tpl * nimg, ids[...].astype(f32), 0.0), axis=1, keepdims=True
    )
    ngrp = group_prec.shape[1]
    grp = lax.broadcasted_iota(jnp.int32, (nimg, ngrp), 1).astype(f32)
    prec = jnp.sum(jnp.where(grp == own_id, group_prec[...], 0.0), axis=1, keepdims=True)

    pl.semaphore_wait(bar, plane - 1 + len(STEPS) + 1)

    def template_copy(q, src_of):
        return remote(tsend.at[rows_of(q)], tbuf.at[rows_of(src_of)], t_s.at[q], t_r.at[src_of], mate(q))

    each(lambda q: template_copy(q, me).start())

    def image_copy(q, src_of):
        return remote(images.at[q], img_buf.at[pix, src_of], i_s.at[q], i_r.at[src_of], mate(q))

    each(lambda q: image_copy(q, me).start())

    def swap(q, h):
        return remote(img_buf.at[h, q], img_buf.at[h, q], x_s.at[q], x_r.at[q], twin)

    own.wait()
    swap(me, pix).start()

    tbuf[rows_of(me), :] = tsend[rows_of(me), :]
    each(lambda q: template_copy(q, q).wait_recv())
    for k in range(tile_rows):
        tall[POS[0], :, k * side : (k + 1) * side] = tbuf[
            pl.ds(k, plane, stride=tile_rows), :
        ].astype(bf16)

    def block(src, dst, step):
        return remote(tall.at[POS[src]], tall.at[POS[dst]], a_s.at[dst], a_r.at[dst], along(step))

    def arrived(dst):
        block(dst, dst, 0).wait_recv()

    moves = [(0, 8, 8), (0, 12, 4), (0, 4, -4)]
    for src in (0, 4, 12, 8):
        moves += [(src, dst, step) for dst, step in RELAY[src]]

    def start_from(src):
        for m in moves:
            if m[0] == src:
                block(*m).start()

    start_from(0)
    middle = plane // 2 + 1

    def pass_image(q):
        image_copy(q, q).wait_recv()
        swap(q, pix).start()

    arrived(4)
    start_from(4)
    arrived(12)
    start_from(12)
    each(pass_image, 1, middle)
    arrived(8)
    start_from(8)
    each(pass_image, middle, plane)
    for k in EARLY:
        if k not in (0, 4, 12):
            arrived(k)
    each(lambda q: swap(q, 1 - pix).wait_recv(), 0, plane)

    def score_copy(h, q, src_of):
        return remote(ssend.at[h, q], srecv.at[h, src_of], s_s.at[h, q], s_r.at[h, src_of], mate(q))

    group = 4

    def score_half(h):
        planes = tall[h * half : (h + 1) * half].reshape(ntpl, 2 * part)
        tf = planes.astype(f32)
        sq = tf * tf
        sq_hi = sq.astype(bf16)
        sq_lo = (sq - sq_hi.astype(f32)).astype(bf16)
        ones = jnp.ones((8, 2 * part), bf16)
        norm = lax.dot_general(ones, sq_hi, NT, preferred_element_type=f32)
        norm += lax.dot_general(ones, sq_lo, NT, preferred_element_type=f32)

        @pl.loop(0, plane // group)
        def _(g):
            at = pl.ds(g * group, group)
            res = jnp.broadcast_to(jnp.zeros((1, 1), f32), (group * nimg, ntpl))
            for c in range(2):
                res += lax.dot_general(
                    img_buf[c, at].reshape(group * nimg, part),
                    tall[h * half : (h + 1) * half, :, c * part : (c + 1) * part].reshape(ntpl, part),
                    NT,
                    preferred_element_type=f32,
                )
            ssend[h, at, :nimg, :] = res.reshape(group, nimg, ntpl)
            ssend[h, at, nimg:, :] = jnp.broadcast_to(norm[None], (group, 8, ntpl))

        each(lambda q: score_copy(h, q, me).start())
        srecv[h, pl.ds(me, 1)] = ssend[h, pl.ds(me, 1)]

    score_half(0)
    for k in LATE:
        if k != 8:
            arrived(k)
    score_half(1)

    def logit_copy(h):
        return remote(lsend.at[h], lrecv.at[h], l_s.at[h], l_r.at[h], twin)

    for h in range(2):
        each(lambda q: score_copy(h, q, q).wait_recv())
        full = jnp.sum(srecv[h], axis=0)
        lsend[h] = prec * full[:nimg] * lax.rsqrt(full[nimg : nimg + 1] + 1e-06)
        logit_copy(h).start()
    own_top = jnp.max(jnp.maximum(lsend[0], lsend[1]), axis=1, keepdims=True)
    for h in range(2):
        logit_copy(h).wait_recv()
    top = jnp.maximum(
        own_top, jnp.max(jnp.maximum(lrecv[0], lrecv[1]), axis=1, keepdims=True)
    )
    weights = [jnp.exp(lsend[h] - top) for h in range(2)]
    totals = jnp.sum(weights[0] + weights[1], axis=1, keepdims=True) + jnp.sum(
        jnp.exp(lrecv[0] - top) + jnp.exp(lrecv[1] - top), axis=1, keepdims=True
    )

    def resp_copy(h, q, src_of):
        return remote(rall.at[h, src_of], rall.at[h, src_of], r_s.at[h, q], r_r.at[h, src_of], mate(q))

    for h in (1, 0):
        rall[h, pl.ds(me, 1)] = (weights[h] / totals).astype(bf16)[None]
        each(lambda q: resp_copy(h, q, me).start())
    column = top + jnp.log(totals)
    eye = lax.broadcasted_iota(jnp.int32, (nimg, nimg), 0) == lax.broadcasted_iota(
        jnp.int32, (nimg, nimg), 1
    )
    loglik[...] = jnp.sum(jnp.where(eye, column, 0.0), axis=0, keepdims=True)

    def near_copy(k, step):
        return remote(sums.at[POS[k]], rr.at[k], z_s.at[k], z_r.at[k], along(step))

    near = {dst: -step for src in RELAY for dst, step in RELAY[src]}

    for h in (1, 0):
        each(lambda q: resp_copy(h, q, q).wait_recv())
        resp = rall[h].reshape(plane * nimg, ntpl).astype(f32).T.astype(bf16)
        for c in range(2):
            res = lax.dot_general(
                resp,
                img_buf[c].reshape(plane * nimg, part),
                (((1,), (0,)), ((), ())),
                preferred_element_type=f32,
            )
            sums[h * half : (h + 1) * half, :, c * part : (c + 1) * part] = res.astype(bf16).reshape(
                half, plane, part
            )
            for k in (0, 4, 8, 12):
                i = POS[k] - h * half
                if 0 <= i < half:
                    own_sums[k // 4, :, c * part : (c + 1) * part] = res[i * plane : (i + 1) * plane]
        for k in ORDER[h * half : (h + 1) * half]:
            if k in near:
                near_copy(k, near[k]).start()

    def far_copy(j):
        return remote(r2_send.at[j], r2_recv.at[j], z2_s.at[j], z2_r.at[j], along(4 * j if j < 3 else -4))

    for j in (2, 1, 3, 0):
        val = own_sums[j]
        for k, step in RELAY[4 * j]:
            near_copy(k, near[k]).wait_recv()
            val = val + rr[k].astype(f32)
        if j > 0:
            r2_send[j] = val.astype(bf16)
            far_copy(j).start()
    for j in (1, 3, 2):
        far_copy(j).wait_recv()
        val = val + r2_recv[j].astype(f32)
    for k in range(tile_rows):
        fsend[pl.ds(k, plane, stride=tile_rows), :] = val[:, k * side : (k + 1) * side]

    def final_copy(q, src_of):
        return remote(fsend.at[rows_of(q)], fin.at[rows_of(src_of)], f_s.at[q], f_r.at[src_of], mate(q))

    each(lambda q: final_copy(q, me).start())
    fin[rows_of(me), :] = fsend[rows_of(me), :]
    each(lambda q: final_copy(q, q).wait_recv())
    whole = fin[...]
    squares = jnp.sum(jnp.sum(whole * whole, axis=0, keepdims=True), axis=1, keepdims=True)
    scaled = whole * lax.rsqrt(squares / (side * side) + 1e-06)
    for q in range(plane):
        for h in range(2):
            at = q * tile_rows + h * part_rows
            stage[h, q * part_rows : (q + 1) * part_rows, :] = scaled[at : at + part_rows, :]
    half_copy = remote(stage.at[1 - pix], orecv, o_s, o_r, twin)
    half_copy.start()
    out[pl.ds(pix, 1)] = stage[pl.ds(pix, 1)]

    each(lambda q: image_copy(q, me).wait_send())
    each(lambda q: swap(q, pix).wait_send(), 0, plane)
    each(lambda q: template_copy(q, me).wait_send())
    for m in moves:
        block(*m).wait_send()
    for h in range(2):
        each(lambda q: score_copy(h, q, me).wait_send())
        each(lambda q: resp_copy(h, q, me).wait_send())
        logit_copy(h).wait_send()
    for k in near:
        near_copy(k, near[k]).wait_send()
    for j in (1, 2, 3):
        far_copy(j).wait_send()
    each(lambda q: final_copy(q, me).wait_send())
    half_copy.wait_recv()
    out[pl.ds(1 - pix, 1)] = orecv[...][None]
    half_copy.wait_send()


def on_device(
    images,
    conformers,
    atom_types,
    type_amp,
    type_width,
    view_angles,
    template_conf,
    template_view,
    group_ids,
    group_prec,
):
    nimg, half_rows, side = images.shape
    plane = NX * NY
    part = half_rows * side // plane
    half = NZ // 2
    ntpl = half * plane
    parts = images.reshape(nimg, plane, part).transpose(1, 0, 2)
    bf16, f32 = jnp.bfloat16, jnp.float32
    vmem = pl.BlockSpec(memory_space=pltpu.VMEM)
    smem = pl.BlockSpec(memory_space=pltpu.SMEM)
    dma = pltpu.SemaphoreType.DMA
    natoms = atom_types.shape[0]
    averages, loglik = pl.pallas_call(
        functools.partial(em_kernel, side, min(512, natoms)),
        out_shape=(
            jax.ShapeDtypeStruct((2, half_rows, side), f32),
            jax.ShapeDtypeStruct((1, nimg), f32),
        ),
        in_specs=[smem] * 4 + [vmem] * 6,
        out_specs=(vmem, vmem),
        scratch_shapes=[
            pltpu.VMEM((2, plane, nimg, part), bf16),
            pltpu.VMEM((side, side), f32),
            pltpu.VMEM((side, side), f32),
            pltpu.VMEM((NZ, plane, 2 * part), bf16),
            pltpu.VMEM((2, plane, nimg + 8, ntpl), f32),
            pltpu.VMEM((2, plane, nimg + 8, ntpl), f32),
            pltpu.VMEM((2, nimg, ntpl), f32),
            pltpu.VMEM((2, nimg, ntpl), f32),
            pltpu.VMEM((2, plane, nimg, ntpl), bf16),
            pltpu.VMEM((4, plane, 2 * part), f32),
            pltpu.VMEM((NZ, plane, 2 * part), bf16),
            pltpu.VMEM((NZ, plane, 2 * part), bf16),
            pltpu.VMEM((4, plane, 2 * part), bf16),
            pltpu.VMEM((4, plane, 2 * part), bf16),
            pltpu.VMEM((side, side), f32),
            pltpu.VMEM((side, side), f32),
            pltpu.VMEM((2, half_rows, side), f32),
            pltpu.VMEM((half_rows, side), f32),
            pltpu.VMEM((side, side), f32),
            dma((plane,)),
            dma((plane,)),
            dma((plane,)),
            dma((plane,)),
            dma((plane,)),
            dma((plane,)),
            dma((NZ,)),
            dma((NZ,)),
            dma((2, plane)),
            dma((2, plane)),
            dma((2,)),
            dma((2,)),
            dma((2, plane)),
            dma((2, plane)),
            dma((NZ,)),
            dma((NZ,)),
            dma((4,)),
            dma((4,)),
            dma((plane,)),
            dma((plane,)),
            dma,
            dma,
            dma,
        ],
        compiler_params=pltpu.CompilerParams(
            collective_id=0, has_side_effects=True, vmem_limit_bytes=56 * 1024 * 1024
        ),
    )(
        template_conf,
        template_view,
        type_amp,
        type_width,
        parts,
        conformers,
        atom_types[None, :],
        view_angles,
        group_ids[None, :],
        group_prec[None, :],
    )
    return averages, loglik[0]


def solution(mesh):
    placed = (
        P(("img", "tpl"), "pix", None),
        P(),
        P(),
        P(),
        P(),
        P(),
        P(("tpl", "img")),
        P(("tpl", "img")),
        P("img"),
        P(),
    )
    return jax.shard_map(
        on_device,
        mesh=mesh,
        in_specs=placed,
        out_specs=(P(("tpl", "img"), "pix", None), P(("img", "tpl"))),
        check_vma=False,
    )
```

time: 127 us -> 98.4 us (0.77)
  Pallas kernels: 112 us -> 90.4 us
  between operations: 6.93 us -> 0.66 us
  other arithmetic: 2.24 us -> 0 us
    pallas_call x1, Pallas kernels: 112 us -> 90.4 us  [on_device(): pl.pallas_call(functools.partial(em_kernel, side, min(512, natoms)), out_...]
    reshape x0 -> x2, local copies, waits for them, and re-layouts: none -> 3.25 us  [on_device(): parts = images.reshape(nimg, plane, part).transpose(1, 0, 2)]
    dynamic_slice x2 -> x0, local copies, waits for them, and re-layouts: 2.09 us -> none  [the longest x1 1.25 us: on_device(): lax.dynamic_index_in_dim(template_view, pix, keepdims=False)]
    unnamed x13 -> x10, local copies, waits for them, and re-layouts: 3.26 us -> 3.87 us
where the time goes in v2:
time: 98.4 us; the launch traced here: 98.2 us
  Pallas kernels  90.4 us (92%)
  local copies, waits for them, and re-layouts  7.12 us (7%)
    pallas_call x1, Pallas kernels, on_device(): pl.pallas_call(functools.partial(em_kernel, side, min(512, natoms)), out_...  90.4 us
    unnamed x10, local copies, waits for them, and re-layouts  3.87 us
    reshape x2, local copies, waits for them, and re-layouts, on_device(): parts = images.reshape(nimg, plane, part).transpose(1, 0, 2)  3.25 us

profile of v2, /device:TPU:1, one launch (start us, length us, event | category | flops | bytes accessed | tf_op | source)
XLA Modules:
  0.0 98.2 jit_solution(10608675107224718137)
XLA Ops:
  0.6 1.7 %reshape.7 = bf16[64,16,512]{2,1,0:T(8,128)(2,1)S(1)} reshape(bf16[64,64,128]{2,1,0:T(8,128)(2,1)} %param.10) | data formatting | bytes 2097152 | tf_op jit(solution)/shard_map/reshape | solution.py:421
  2.3 0.0 copy-start
  2.4 1.5 %copy.18 = bf16[64,16,512]{2,0,1:T(8,128)(2,1)} copy(bf16[64,16,512]{2,1,0:T(8,128)(2,1)S(1)} %reshape.7) | data formatting | bytes 2097152 | tf_op jit(solution)/shard_map/reshape | solution.py:421
  3.9 0.0 copy-done
  3.9 0.0 copy-start.1
  3.9 1.1 %copy.15.conformers = f32[8,3,4096]{2,1,0:T(4,128)} copy(f32[8,3,4096]{2,0,1:T(8,128)S(1)} %copy-done) | data formatting | bytes 786432 | tf_op args[1]
  5.0 0.0 copy-done.1
  5.0 0.8 copy.16.angles
  5.8 90.4 %shard_map.113 = (f32[2,64,128]{2,1,0:T(8,128)}, f32[1,64]{1,0:T(1,128)}) custom-call(s32[2]{0:T(128)} %conf_sm.1, s32[2]{0:T(128)} %view_sm.1, f32[5]{0:T(128)} %tamp_sm.1, f32[5]{0:T(128)} %twid_sm.1, bf16[16,64,512]{2,1,0:T(8,128)(2,1)} %bitcast.7, f32[8,3,4096]{2,1,0:T(4,128)} %copy.15.conformers, s32[1,4096]{1,0:T(1,128)} %bitcast.8, ...), custom_call_target="tpu_custom_call" | custom-call | tf_op jit(solution)/shard_map/pallas_call | solution.py:427
  96.2 0.0 copy-start.2
  96.2 1.5 %copy.21 = f32[2,64,128]{2,1,0:T(8,128)} copy(f32[2,64,128]{2,1,0:T(8,128)} %get-tuple-element.8) | data formatting | bytes 131072
  97.7 0.0 copy-done.2
  97.7 0.5 copy.22
Async XLA Ops:
  2.3 1.6 %copy-start = (f32[8,3,4096]{2,0,1:T(8,128)S(1)}, f32[8,3,4096]{2,0,1:T(8,128)}, u32[]{:S(2)}) copy-start(f32[8,3,4096]{2,0,1:T(8,128)} %param.11) | copy-start | bytes 1179652
  3.9 1.1 %copy-start.1 = (f32[256,3]{0,1:T(4,128)S(1)}, f32[256,3]{0,1:T(4,128)}, u32[]{:S(2)}) copy-start(f32[256,3]{0,1:T(4,128)} %param.15) | copy-start | bytes 9220
  96.2 1.5 %copy-start.2 = (f32[1,64]{1,0:T(1,128)S(1)}, f32[1,64]{1,0:T(1,128)}, u32[]{:S(2)}) copy-start(f32[1,64]{1,0:T(1,128)} %get-tuple-element.5) | copy-start | bytes 772

commit v3 on v2

--- a/solution.py
+++ b/solution.py
@@ -18,7 +18,9 @@
 POS = {k: i for i, k in enumerate(ORDER)}
 NZ = 16
 RELAY = {0: ((1, -1), (15, 1), (2, -2), (14, 2)), 4: ((5, -1), (3, 1), (6, -2)), 12: ((13, -1), (11, 1), (10, 2)), 8: ((9, -1), (7, 1))}
-STEPS = (1, -1, 2, -2, 4, -4, 8)
+OWN_MOVES = ((0, 8, 8), (0, 12, 4), (0, 4, -4), (0, 3, -3), (0, 1, -1), (0, 15, 1), (0, 2, -2), (0, 14, 2))
+RELAY_MOVES = {4: ((4, 5, -1), (4, 6, -2)), 12: ((12, 13, -1), (12, 11, 1), (12, 10, 2)), 8: ((8, 9, -1), (8, 7, 1))}
+STEPS = (1, -1, 2, -2, 3, -3, 4, -4, 8)
 
 
 def em_kernel(
@@ -96,6 +98,8 @@
     nimg = images.shape[1]
     half = len(EARLY)
     ntpl = half * plane
+    full = 2 * part
+    tile = 2 * tile_rows
 
     def mate(q):
         qy = lax.div(q, NX)
@@ -113,13 +117,19 @@
     def rows_of(q):
         return pl.ds(pl.multiple_of(q * tile_rows, tile_rows), tile_rows)
 
+    def tile_of(q):
+        return pl.ds(pl.multiple_of(q * tile, tile), tile)
+
+    def slot(q):
+        return lax.rem(q, 2) * (plane // 2) + lax.div(q, 2)
+
     def remote(src, dst, ss, rs, dev):
         return pltpu.make_async_remote_copy(
             src_ref=src, dst_ref=dst, send_sem=ss, recv_sem=rs, device_id=dev, device_id_type=MESH
         )
 
-    def each(body, first=1, last=plane):
-        @pl.loop(first, last)
+    def each(body, first=1, last=plane, step=1):
+        @pl.loop(first, last, step=step)
         def _(d):
             body(lax.rem(me + d, plane))
 
@@ -129,7 +139,7 @@
         pl.semaphore_signal(bar, inc=1, device_id=along(step), device_id_type=MESH)
     pl.semaphore_signal(bar, inc=1, device_id=twin, device_id_type=MESH)
 
-    own = pltpu.make_async_copy(images.at[me], img_buf.at[pix, me], own_sem)
+    own = pltpu.make_async_copy(images.at[me], img_buf.at[pix, slot(me)], own_sem)
     own.start()
 
     conf = conf_sm[pix]
@@ -181,7 +191,12 @@
         total += lax.dot_general(row_hi, col_hi, NT, preferred_element_type=f32)
         acc[...] += total
 
-    tsend[...] = acc[...].astype(bf16).astype(f32)
+    rendered = acc[...].astype(bf16).astype(f32)
+    square = rendered * rendered
+    norm = jnp.sum(jnp.sum(square, axis=0, keepdims=True), axis=1, keepdims=True)
+    for q in range(plane):
+        tsend[q * tile : q * tile + tile_rows, :] = rendered[q * tile_rows : (q + 1) * tile_rows, :]
+        tsend[q * tile + tile_rows : (q + 1) * tile, :] = jnp.broadcast_to(norm, (tile_rows, side))
 
     groups = ids.shape[1]
     at_row = lax.broadcasted_iota(jnp.int32, (nimg, groups), 0)
@@ -196,27 +211,36 @@
     pl.semaphore_wait(bar, plane - 1 + len(STEPS) + 1)
 
     def template_copy(q, src_of):
-        return remote(tsend.at[rows_of(q)], tbuf.at[rows_of(src_of)], t_s.at[q], t_r.at[src_of], mate(q))
+        return remote(tsend.at[tile_of(q)], tbuf.at[tile_of(src_of)], t_s.at[q], t_r.at[src_of], mate(q))
 
     each(lambda q: template_copy(q, me).start())
 
     def image_copy(q, src_of):
-        return remote(images.at[q], img_buf.at[pix, src_of], i_s.at[q], i_r.at[src_of], mate(q))
-
-    each(lambda q: image_copy(q, me).start())
+        return remote(
+            images.at[q], img_buf.at[pix, slot(src_of)], i_s.at[q], i_r.at[src_of], mate(q)
+        )
+
+    each(lambda q: image_copy(q, me).start(), 1, plane, 2)
 
     def swap(q, h):
-        return remote(img_buf.at[h, q], img_buf.at[h, q], x_s.at[q], x_r.at[q], twin)
+        return remote(img_buf.at[h, slot(q)], img_buf.at[h, slot(q)], x_s.at[q], x_r.at[q], twin)
 
     own.wait()
     swap(me, pix).start()
 
-    tbuf[rows_of(me), :] = tsend[rows_of(me), :]
+    tbuf[tile_of(me), :] = tsend[tile_of(me), :]
     each(lambda q: template_copy(q, q).wait_recv())
     for k in range(tile_rows):
         tall[POS[0], :, k * side : (k + 1) * side] = tbuf[
-            pl.ds(k, plane, stride=tile_rows), :
+            pl.ds(k, plane, stride=tile), :
         ].astype(bf16)
+    norms = tbuf[pl.ds(tile_rows, plane, stride=tile), :]
+    first = norms.astype(bf16).astype(f32)
+    second = (norms - first).astype(bf16).astype(f32)
+    third = norms - first - second
+    lane = lax.broadcasted_iota(jnp.int32, (plane, side), 1)
+    pieces = jnp.where(lane == 0, first, jnp.where(lane == 1, second, jnp.where(lane == 2, third, 0.0)))
+    tall[POS[0], :, full:] = pieces.astype(bf16)
 
     def block(src, dst, step):
         return remote(tall.at[POS[src]], tall.at[POS[dst]], a_s.at[dst], a_r.at[dst], along(step))
@@ -224,54 +248,33 @@
     def arrived(dst):
         block(dst, dst, 0).wait_recv()
 
-    moves = [(0, 8, 8), (0, 12, 4), (0, 4, -4)]
-    for src in (0, 4, 12, 8):
-        moves += [(src, dst, step) for dst, step in RELAY[src]]
-
-    def start_from(src):
-        for m in moves:
-            if m[0] == src:
-                block(*m).start()
-
-    start_from(0)
-    middle = plane // 2 + 1
+    def relay(k):
+        arrived(k)
+        for m in RELAY_MOVES[k]:
+            block(*m).start()
+
+    for m in OWN_MOVES:
+        block(*m).start()
+    each(lambda q: image_copy(q, me).start(), 2, plane, 2)
 
     def pass_image(q):
         image_copy(q, q).wait_recv()
         swap(q, pix).start()
 
-    arrived(4)
-    start_from(4)
-    arrived(12)
-    start_from(12)
-    each(pass_image, 1, middle)
-    arrived(8)
-    start_from(8)
-    each(pass_image, middle, plane)
-    for k in EARLY:
-        if k not in (0, 4, 12):
-            arrived(k)
-    each(lambda q: swap(q, 1 - pix).wait_recv(), 0, plane)
-
     def score_copy(h, q, src_of):
-        return remote(ssend.at[h, q], srecv.at[h, src_of], s_s.at[h, q], s_r.at[h, src_of], mate(q))
+        return remote(
+            ssend.at[h, slot(q)], srecv.at[h, slot(src_of)], s_s.at[h, q], s_r.at[h, src_of], mate(q)
+        )
 
     group = 4
 
-    def score_half(h):
-        planes = tall[h * half : (h + 1) * half].reshape(ntpl, 2 * part)
-        tf = planes.astype(f32)
-        sq = tf * tf
-        sq_hi = sq.astype(bf16)
-        sq_lo = (sq - sq_hi.astype(f32)).astype(bf16)
-        ones = jnp.ones((8, 2 * part), bf16)
-        norm = lax.dot_general(ones, sq_hi, NT, preferred_element_type=f32)
-        norm += lax.dot_general(ones, sq_lo, NT, preferred_element_type=f32)
-
-        @pl.loop(0, plane // group)
+    def score_part(h, odd):
+        base = lax.rem(me + odd, 2) * (plane // 2)
+
+        @pl.loop(0, plane // 2 // group)
         def _(g):
-            at = pl.ds(g * group, group)
-            res = jnp.broadcast_to(jnp.zeros((1, 1), f32), (group * nimg, ntpl))
+            at = pl.ds(base + g * group, group)
+            res = jnp.zeros((group * nimg, ntpl), f32)
             for c in range(2):
                 res += lax.dot_general(
                     img_buf[c, at].reshape(group * nimg, part),
@@ -279,25 +282,44 @@
                     NT,
                     preferred_element_type=f32,
                 )
-            ssend[h, at, :nimg, :] = res.reshape(group, nimg, ntpl)
-            ssend[h, at, nimg:, :] = jnp.broadcast_to(norm[None], (group, 8, ntpl))
-
-        each(lambda q: score_copy(h, q, me).start())
-        srecv[h, pl.ds(me, 1)] = ssend[h, pl.ds(me, 1)]
-
-    score_half(0)
+            ssend[h, at] = res.reshape(group, nimg, ntpl)
+
+        each(lambda q: score_copy(h, q, me).start(), 2 - odd, plane, 2)
+
+    each(pass_image, 1, plane, 2)
+    relay(4)
+    relay(12)
+    for k in EARLY:
+        if k not in (0, 4, 12):
+            arrived(k)
+    each(lambda q: swap(q, 1 - pix).wait_recv(), 1, plane, 2)
+    score_part(0, 1)
+    relay(8)
+    each(pass_image, 2, plane, 2)
+    each(lambda q: swap(q, 1 - pix).wait_recv(), 0, plane, 2)
+    score_part(0, 0)
     for k in LATE:
         if k != 8:
             arrived(k)
-    score_half(1)
+    score_part(1, 1)
+    score_part(1, 0)
+    for h in range(2):
+        srecv[h, pl.ds(slot(me), 1)] = ssend[h, pl.ds(slot(me), 1)]
 
     def logit_copy(h):
         return remote(lsend.at[h], lrecv.at[h], l_s.at[h], l_r.at[h], twin)
 
+    chosen = (lax.broadcasted_iota(jnp.int32, (8, side), 1) < 3).astype(f32).astype(bf16)
     for h in range(2):
+        norm = lax.dot_general(
+            chosen,
+            tall[h * half : (h + 1) * half, :, full:].reshape(ntpl, side),
+            NT,
+            preferred_element_type=f32,
+        )
+        gain = prec * lax.rsqrt(norm[:1] + 1e-06)
         each(lambda q: score_copy(h, q, q).wait_recv())
-        full = jnp.sum(srecv[h], axis=0)
-        lsend[h] = prec * full[:nimg] * lax.rsqrt(full[nimg : nimg + 1] + 1e-06)
+        lsend[h] = gain * jnp.sum(srecv[h], axis=0)
         logit_copy(h).start()
     own_top = jnp.max(jnp.maximum(lsend[0], lsend[1]), axis=1, keepdims=True)
     for h in range(2):
@@ -311,10 +333,12 @@
     )
 
     def resp_copy(h, q, src_of):
-        return remote(rall.at[h, src_of], rall.at[h, src_of], r_s.at[h, q], r_r.at[h, src_of], mate(q))
+        return remote(
+            rall.at[h, slot(src_of)], rall.at[h, slot(src_of)], r_s.at[h, q], r_r.at[h, src_of], mate(q)
+        )
 
     for h in (1, 0):
-        rall[h, pl.ds(me, 1)] = (weights[h] / totals).astype(bf16)[None]
+        rall[h, pl.ds(slot(me), 1)] = (weights[h] / totals).astype(bf16)[None]
         each(lambda q: resp_copy(h, q, me).start())
     column = top + jnp.log(totals)
     eye = lax.broadcasted_iota(jnp.int32, (nimg, nimg), 0) == lax.broadcasted_iota(
@@ -385,7 +409,7 @@
     each(lambda q: image_copy(q, me).wait_send())
     each(lambda q: swap(q, pix).wait_send(), 0, plane)
     each(lambda q: template_copy(q, me).wait_send())
-    for m in moves:
+    for m in OWN_MOVES + RELAY_MOVES[4] + RELAY_MOVES[12] + RELAY_MOVES[8]:
         block(*m).wait_send()
     for h in range(2):
         each(lambda q: score_copy(h, q, me).wait_send())
@@ -434,11 +458,11 @@
         out_specs=(vmem, vmem),
         scratch_shapes=[
             pltpu.VMEM((2, plane, nimg, part), bf16),
-            pltpu.VMEM((side, side), f32),
-            pltpu.VMEM((side, side), f32),
-            pltpu.VMEM((NZ, plane, 2 * part), bf16),
-            pltpu.VMEM((2, plane, nimg + 8, ntpl), f32),
-            pltpu.VMEM((2, plane, nimg + 8, ntpl), f32),
+            pltpu.VMEM((2 * side, side), f32),
+            pltpu.VMEM((2 * side, side), f32),
+            pltpu.VMEM((NZ, plane, 2 * part + side), bf16),
+            pltpu.VMEM((2, plane, nimg, ntpl), f32),
+            pltpu.VMEM((2, plane, nimg, ntpl), f32),
             pltpu.VMEM((2, nimg, ntpl), f32),
             pltpu.VMEM((2, nimg, ntpl), f32),
             pltpu.VMEM((2, plane, nimg, ntpl), bf16),
@@ -477,7 +501,7 @@
             dma,
         ],
         compiler_params=pltpu.CompilerParams(
-            collective_id=0, has_side_effects=True, vmem_limit_bytes=56 * 1024 * 1024
+            collective_id=0, has_side_effects=True, vmem_limit_bytes=28 * 1024 * 1024
         ),
     )(
         template_conf,

time: 98.4 us -> 89.1 us (0.905)
  Pallas kernels: 90.4 us -> 82.3 us
  local copies, waits for them, and re-layouts: 7.12 us -> 5.33 us
    pallas_call x1, Pallas kernels: 90.4 us -> 82.3 us  [on_device(): pl.pallas_call(functools.partial(em_kernel, side, min(512, natoms)), out_...]
    unnamed x10 -> x22, local copies, waits for them, and re-layouts: 3.87 us -> 3.04 us
where the time goes in v3:
time: 89.1 us; the launch traced here: 88.4 us
  Pallas kernels  82.3 us (92%)
  local copies, waits for them, and re-layouts  5.33 us (6%)
    pallas_call x1, Pallas kernels, on_device(): pl.pallas_call(functools.partial(em_kernel, side, min(512, natoms)), out_...  82.3 us
    unnamed x22, local copies, waits for them, and re-layouts  3.04 us
    reshape x2, local copies, waits for them, and re-layouts, on_device(): parts = images.reshape(nimg, plane, part).transpose(1, 0, 2)  2.28 us

profile of v3, /device:TPU:1, one launch (start us, length us, event | category | flops | bytes accessed | tf_op | source)
XLA Modules:
  0.0 88.4 jit_solution(4372211355632316116)
XLA Ops:
  0.6 1.7 %reshape.7 = bf16[64,16,512]{2,1,0:T(8,128)(2,1)S(1)} reshape(bf16[64,64,128]{2,1,0:T(8,128)(2,1)} %param.10) | data formatting | bytes 2097152 | tf_op jit(solution)/shard_map/reshape | solution.py:445
  2.3 0.0 copy-start.7
  2.4 0.6 copy.18
  2.9 0.4 copy-done.7
  3.3 0.0 copy-start.8
  3.3 0.3 copy.15.conformers
  3.6 0.4 copy-done.8
  4.0 0.0 copy-start
  4.0 0.0 copy-start.2
  4.0 0.0 copy-start.4
  4.0 0.0 copy-start.5
  4.0 0.0 copy-start.6
  4.0 0.1 copy.16.angles
  4.2 0.0 copy-start.1
  4.2 0.0 copy-start.3
  4.2 0.5 copy-done
  4.7 0.0 copy-done.2
  4.7 0.0 copy-done.4
  4.7 0.0 copy-done.5
  4.8 0.0 copy-done.6
  4.8 0.1 copy-done.1
  4.9 0.0 copy-done.3
  4.9 82.3 %shard_map.113 = (f32[2,64,128]{2,1,0:T(8,128)S(1)}, f32[1,64]{1,0:T(1,128)S(1)}) custom-call(s32[2]{0:T(128)S(1)} %copy-done.3, s32[2]{0:T(128)S(1)} %copy-done.4, f32[5]{0:T(128)S(1)} %copy-done.5, f32[5]{0:T(128)S(1)} %copy-done.6, bf16[16,64,512]{2,1,0:T(8,128)(2,1)S(1)} %bitcast.7, f32[8,3,4096]{2,1,0:T(4,128)S(1)} %copy.15.conformers, ...), custom_call_target="tpu_custom_call" | custom-call | tf_op jit(solution)/shard_map/pallas_call | solution.py:451
  87.2 0.6 copy.21
  87.8 0.5 copy.22
Async XLA Ops:
  2.3 1.0 %copy-start.7 = (f32[8,3,4096]{2,0,1:T(8,128)S(1)}, f32[8,3,4096]{2,0,1:T(8,128)}, u32[]{:S(2)}) copy-start(f32[8,3,4096]{2,0,1:T(8,128)} %param.11) | copy-start | bytes 1179652
  3.3 0.7 copy-start.8
  4.0 0.7 copy-start
  4.0 0.7 copy-start.2
  4.0 0.7 copy-start.4
  4.0 0.7 copy-start.5
  4.0 0.7 copy-start.6
  4.2 0.7 copy-start.1
  4.2 0.7 copy-start.3

commit v4 on v3

--- a/solution.py
+++ b/solution.py
@@ -12,15 +12,24 @@
 NT = (((1,), (1,)), ((), ()))
 
 
-EARLY = (0, 1, 2, 3, 4, 12, 14, 15)
-LATE = (8, 7, 9, 5, 6, 10, 11, 13)
+EARLY = (0, 1, 2, 5, 11, 13, 14, 15)
+LATE = (8, 3, 7, 9, 4, 6, 10, 12)
 ORDER = EARLY + LATE
 POS = {k: i for i, k in enumerate(ORDER)}
 NZ = 16
-RELAY = {0: ((1, -1), (15, 1), (2, -2), (14, 2)), 4: ((5, -1), (3, 1), (6, -2)), 12: ((13, -1), (11, 1), (10, 2)), 8: ((9, -1), (7, 1))}
-OWN_MOVES = ((0, 8, 8), (0, 12, 4), (0, 4, -4), (0, 3, -3), (0, 1, -1), (0, 15, 1), (0, 2, -2), (0, 14, 2))
-RELAY_MOVES = {4: ((4, 5, -1), (4, 6, -2)), 12: ((12, 13, -1), (12, 11, 1), (12, 10, 2)), 8: ((8, 9, -1), (8, 7, 1))}
-STEPS = (1, -1, 2, -2, 3, -3, 4, -4, 8)
+RELAY = {
+    0: ((1, -1), (15, 1), (2, -2), (14, 2)),
+    5: ((8, -3), (3, 2), (7, -2), (4, 1), (6, -1)),
+    11: ((13, -2), (9, 2), (10, 1), (12, -1)),
+}
+FAR = {5: 5, 11: -5}
+BASE = {k: i for i, k in enumerate(RELAY)}
+OWN_MOVES = ((0, 11, 5), (0, 5, -5), (0, 13, 3), (0, 1, -1), (0, 15, 1), (0, 2, -2), (0, 14, 2))
+RELAY_MOVES = {
+    5: ((5, 8, -3), (5, 3, 2), (5, 7, -2), (5, 4, 1), (5, 6, -1)),
+    11: ((11, 9, 2), (11, 10, 1), (11, 12, -1)),
+}
+STEPS = (1, -1, 2, -2, 3, -3, 5, -5)
 
 
 def em_kernel(
@@ -95,7 +104,7 @@
     part_rows = half_rows // plane
     part = part_rows * side
     tile_rows = 2 * part_rows
-    nimg = images.shape[1]
+    nimg = images.shape[0]
     half = len(EARLY)
     ntpl = half * plane
     full = 2 * part
@@ -139,15 +148,19 @@
         pl.semaphore_signal(bar, inc=1, device_id=along(step), device_id_type=MESH)
     pl.semaphore_signal(bar, inc=1, device_id=twin, device_id_type=MESH)
 
-    own = pltpu.make_async_copy(images.at[me], img_buf.at[pix, slot(me)], own_sem)
+    def image_part(q):
+        return images.at[:, pl.ds(pl.multiple_of(q * part, part), part)]
+
+    own = pltpu.make_async_copy(image_part(me), img_buf.at[pix, slot(me)], own_sem)
     own.start()
 
     conf = conf_sm[pix]
-    view = angles[pl.ds(view_sm[pix], 1), :]
+    views = lax.broadcasted_iota(jnp.int32, angles.shape, 1)
+    view = jnp.sum(jnp.where(views == view_sm[pix], angles[...], 0.0), axis=1, keepdims=True)
     cosines = jnp.cos(view)
     sines = jnp.sin(view)
-    cos_phi, cos_theta, cos_psi = (cosines[:, i : i + 1] for i in range(3))
-    sin_phi, sin_theta, sin_psi = (sines[:, i : i + 1] for i in range(3))
+    cos_phi, cos_theta, cos_psi = (cosines[i : i + 1, :] for i in range(3))
+    sin_phi, sin_theta, sin_psi = (sines[i : i + 1, :] for i in range(3))
     r00 = cos_phi * cos_theta * cos_psi - sin_phi * sin_psi
     r01 = -cos_phi * cos_theta * sin_psi - sin_phi * cos_psi
     r02 = cos_phi * sin_theta
@@ -173,9 +186,7 @@
             width = jnp.where(kind == j, twid_sm[j], width)
         amp = amp * 0.0625
         spread = 0.5 / (width * width)
-        c0 = conformers[conf, 0:1, sl]
-        c1 = conformers[conf, 1:2, sl]
-        c2 = conformers[conf, 2:3, sl]
+        c0, c1, c2 = (conformers[i, pl.ds(conf, 1), sl] for i in range(3))
         across = r00 * c0 + r01 * c1 + r02 * c2
         below = r10 * c0 + r11 * c1 + r12 * c2
         dc = col_pos - across
@@ -217,7 +228,7 @@
 
     def image_copy(q, src_of):
         return remote(
-            images.at[q], img_buf.at[pix, slot(src_of)], i_s.at[q], i_r.at[src_of], mate(q)
+            image_part(q), img_buf.at[pix, slot(src_of)], i_s.at[q], i_r.at[src_of], mate(q)
         )
 
     each(lambda q: image_copy(q, me).start(), 1, plane, 2)
@@ -287,20 +298,18 @@
         each(lambda q: score_copy(h, q, me).start(), 2 - odd, plane, 2)
 
     each(pass_image, 1, plane, 2)
-    relay(4)
-    relay(12)
+    relay(5)
+    relay(11)
     for k in EARLY:
-        if k not in (0, 4, 12):
+        if k not in BASE:
             arrived(k)
     each(lambda q: swap(q, 1 - pix).wait_recv(), 1, plane, 2)
     score_part(0, 1)
-    relay(8)
     each(pass_image, 2, plane, 2)
     each(lambda q: swap(q, 1 - pix).wait_recv(), 0, plane, 2)
     score_part(0, 0)
     for k in LATE:
-        if k != 8:
-            arrived(k)
+        arrived(k)
     score_part(1, 1)
     score_part(1, 0)
     for h in range(2):
@@ -351,6 +360,21 @@
 
     near = {dst: -step for src in RELAY for dst, step in RELAY[src]}
 
+    def far_copy(b):
+        j = BASE[b]
+        return remote(r2_send.at[j], r2_recv.at[j], z2_s.at[j], z2_r.at[j], along(FAR[b]))
+
+    def base_sum(b):
+        val = own_sums[BASE[b]]
+        for k, step in RELAY[b]:
+            near_copy(k, near[k]).wait_recv()
+            val = val + rr[k].astype(f32)
+        return val
+
+    def send_far(b):
+        r2_send[BASE[b]] = base_sum(b).astype(bf16)
+        far_copy(b).start()
+
     for h in (1, 0):
         each(lambda q: resp_copy(h, q, q).wait_recv())
         resp = rall[h].reshape(plane * nimg, ntpl).astype(f32).T.astype(bf16)
@@ -364,28 +388,19 @@
             sums[h * half : (h + 1) * half, :, c * part : (c + 1) * part] = res.astype(bf16).reshape(
                 half, plane, part
             )
-            for k in (0, 4, 8, 12):
+            for k in BASE:
                 i = POS[k] - h * half
                 if 0 <= i < half:
-                    own_sums[k // 4, :, c * part : (c + 1) * part] = res[i * plane : (i + 1) * plane]
-        for k in ORDER[h * half : (h + 1) * half]:
+                    own_sums[BASE[k], :, c * part : (c + 1) * part] = res[i * plane : (i + 1) * plane]
+        for k in (ORDER[half:] if h else (13, 2, 14, 1, 15)):
             if k in near:
                 near_copy(k, near[k]).start()
-
-    def far_copy(j):
-        return remote(r2_send.at[j], r2_recv.at[j], z2_s.at[j], z2_r.at[j], along(4 * j if j < 3 else -4))
-
-    for j in (2, 1, 3, 0):
-        val = own_sums[j]
-        for k, step in RELAY[4 * j]:
-            near_copy(k, near[k]).wait_recv()
-            val = val + rr[k].astype(f32)
-        if j > 0:
-            r2_send[j] = val.astype(bf16)
-            far_copy(j).start()
-    for j in (1, 3, 2):
-        far_copy(j).wait_recv()
-        val = val + r2_recv[j].astype(f32)
+    for b in FAR:
+        send_far(b)
+    val = base_sum(0)
+    for b in FAR:
+        far_copy(b).wait_recv()
+        val = val + r2_recv[BASE[b]].astype(f32)
     for k in range(tile_rows):
         fsend[pl.ds(k, plane, stride=tile_rows), :] = val[:, k * side : (k + 1) * side]
 
@@ -409,7 +424,7 @@
     each(lambda q: image_copy(q, me).wait_send())
     each(lambda q: swap(q, pix).wait_send(), 0, plane)
     each(lambda q: template_copy(q, me).wait_send())
-    for m in OWN_MOVES + RELAY_MOVES[4] + RELAY_MOVES[12] + RELAY_MOVES[8]:
+    for m in OWN_MOVES + RELAY_MOVES[5] + RELAY_MOVES[11]:
         block(*m).wait_send()
     for h in range(2):
         each(lambda q: score_copy(h, q, me).wait_send())
@@ -417,8 +432,8 @@
         logit_copy(h).wait_send()
     for k in near:
         near_copy(k, near[k]).wait_send()
-    for j in (1, 2, 3):
-        far_copy(j).wait_send()
+    for b in FAR:
+        far_copy(b).wait_send()
     each(lambda q: final_copy(q, me).wait_send())
     half_copy.wait_recv()
     out[pl.ds(1 - pix, 1)] = orecv[...][None]
@@ -442,7 +457,7 @@
     part = half_rows * side // plane
     half = NZ // 2
     ntpl = half * plane
-    parts = images.reshape(nimg, plane, part).transpose(1, 0, 2)
+    flat = images.reshape(nimg, half_rows * side)
     bf16, f32 = jnp.bfloat16, jnp.float32
     vmem = pl.BlockSpec(memory_space=pltpu.VMEM)
     smem = pl.BlockSpec(memory_space=pltpu.SMEM)
@@ -466,11 +481,11 @@
             pltpu.VMEM((2, nimg, ntpl), f32),
             pltpu.VMEM((2, nimg, ntpl), f32),
             pltpu.VMEM((2, plane, nimg, ntpl), bf16),
-            pltpu.VMEM((4, plane, 2 * part), f32),
+            pltpu.VMEM((len(RELAY), plane, 2 * part), f32),
             pltpu.VMEM((NZ, plane, 2 * part), bf16),
             pltpu.VMEM((NZ, plane, 2 * part), bf16),
-            pltpu.VMEM((4, plane, 2 * part), bf16),
-            pltpu.VMEM((4, plane, 2 * part), bf16),
+            pltpu.VMEM((len(RELAY), plane, 2 * part), bf16),
+            pltpu.VMEM((len(RELAY), plane, 2 * part), bf16),
             pltpu.VMEM((side, side), f32),
             pltpu.VMEM((side, side), f32),
             pltpu.VMEM((2, half_rows, side), f32),
@@ -492,8 +507,8 @@
             dma((2, plane)),
             dma((NZ,)),
             dma((NZ,)),
-            dma((4,)),
-            dma((4,)),
+            dma((len(RELAY),)),
+            dma((len(RELAY),)),
             dma((plane,)),
             dma((plane,)),
             dma,
@@ -508,10 +523,10 @@
         template_view,
         type_amp,
         type_width,
-        parts,
-        conformers,
+        flat,
+        conformers.transpose(1, 0, 2),
         atom_types[None, :],
-        view_angles,
+        view_angles.T,
         group_ids[None, :],
         group_prec[None, :],
     )

time: 89.1 us -> 87.9 us (0.987)
  local copies, waits for them, and re-layouts: 5.33 us -> 3.73 us
  Pallas kernels: 82.3 us -> 83.2 us
    reshape x2 -> x0, local copies, waits for them, and re-layouts: 2.28 us -> none  [on_device(): parts = images.reshape(nimg, plane, part).transpose(1, 0, 2)]
    pallas_call x1, Pallas kernels: 82.3 us -> 83.2 us  [on_device(): pl.pallas_call(functools.partial(em_kernel, side, min(512, natoms)), out_...]
    unnamed x22 -> x21, local copies, waits for them, and re-layouts: 3.04 us -> 3.73 us
where the time goes in v4:
time: 87.9 us; the launch traced here: 87.7 us
  Pallas kernels  83.2 us (95%)
  local copies, waits for them, and re-layouts  3.73 us (4%)
    pallas_call x1, Pallas kernels, on_device(): pl.pallas_call(functools.partial(em_kernel, side, min(512, natoms)), out_...  83.2 us
    unnamed x21, local copies, waits for them, and re-layouts  3.73 us

profile of v4, /device:TPU:1, one launch (start us, length us, event | category | flops | bytes accessed | tf_op | source)
XLA Modules:
  0.0 87.7 jit_solution(16671015943254125449)
XLA Ops:
  0.6 0.0 copy-start
  0.6 0.0 copy-start.1
  0.7 0.0 copy-start.2
  0.7 0.0 copy-start.4
  0.7 0.0 copy-start.6
  0.7 0.0 copy-start.7
  0.7 0.0 copy-start.8
  0.7 2.0 %copy.14 = bf16[8,8,64,128]{3,1,2,0:T(8,128)(2,1)S(1)} copy(bf16[8,8,64,128]{3,2,1,0:T(8,128)(2,1)} %bitcast.17) | data formatting | bytes 2097152
  2.7 0.0 copy-start.3
  2.7 0.0 copy-start.5
  2.7 0.0 copy-done
  2.7 0.0 copy-done.1
  2.7 0.0 copy-done.2
  2.7 0.0 copy-done.4
  2.7 0.0 copy-done.6
  2.7 0.0 copy-done.7
  2.7 0.0 copy-done.8
  2.8 0.6 copy-done.3
  3.3 0.0 copy-done.5
  3.3 83.2 %shard_map.113 = (f32[2,64,128]{2,1,0:T(8,128)S(1)}, f32[1,64]{1,0:T(1,128)S(1)}) custom-call(s32[2]{0:T(128)S(1)} %copy-done.5, s32[2]{0:T(128)S(1)} %copy-done.6, f32[5]{0:T(128)S(1)} %copy-done.7, f32[5]{0:T(128)S(1)} %copy-done.8, bf16[64,8192]{1,0:T(8,128)(2,1)S(1)} %bitcast.10, f32[3,8,4096]{2,1,0:T(8,128)S(1)} %bitcast.11, s32[1,4096]{1,0:T(1,128)S(1)} %bitcast.12, ...), custom_call_target="tpu_custom_call" | custom-call | tf_op jit(solution)/shard_map/pallas_call | solution.py:466
  86.6 0.6 copy.17
  87.2 0.5 copy.18
Async XLA Ops:
  0.6 2.1 %copy-start = (f32[8,3,4096]{2,0,1:T(8,128)S(1)}, f32[8,3,4096]{2,0,1:T(8,128)}, u32[]{:S(2)}) copy-start(f32[8,3,4096]{2,0,1:T(8,128)} %param.11) | copy-start | bytes 1179652
  0.6 2.1 %copy-start.1 = (s32[4096]{0:T(1024)S(1)}, s32[4096]{0:T(1024)}, u32[]{:S(2)}) copy-start(s32[4096]{0:T(1024)} %param.12) | copy-start | bytes 49156
  0.7 2.1 %copy-start.2 = (f32[256,3]{0,1:T(4,128)S(1)}, f32[256,3]{0,1:T(4,128)}, u32[]{:S(2)}) copy-start(f32[256,3]{0,1:T(4,128)} %param.15) | copy-start | bytes 9220
  0.7 2.1 %copy-start.4 = (f32[256]{0:T(256)S(1)}, f32[256]{0:T(256)}, u32[]{:S(2)}) copy-start(f32[256]{0:T(256)} %param.19) | copy-start | bytes 3076
  0.7 2.1 %copy-start.6 = (s32[2]{0:T(128)S(1)}, s32[2]{0:T(128)}, u32[]{:S(2)}) copy-start(s32[2]{0:T(128)} %view_sm.1) | copy-start | bytes 28
  0.7 2.1 %copy-start.7 = (f32[5]{0:T(128)S(1)}, f32[5]{0:T(128)}, u32[]{:S(2)}) copy-start(f32[5]{0:T(128)} %tamp_sm.1) | copy-start | bytes 64
  0.7 2.1 %copy-start.8 = (f32[5]{0:T(128)S(1)}, f32[5]{0:T(128)}, u32[]{:S(2)}) copy-start(f32[5]{0:T(128)} %twid_sm.1) | copy-start | bytes 64
  2.7 0.7 copy-start.3
  2.7 0.7 copy-start.5

commit v5 on v4

--- a/solution.py
+++ b/solution.py
@@ -137,6 +137,11 @@
             src_ref=src, dst_ref=dst, send_sem=ss, recv_sem=rs, device_id=dev, device_id_type=MESH
         )
 
+    def joint(src, dst, ss, rs):
+        return remote(src, dst, ss, rs, twin)
+
+    others = plane - 1
+
     def each(body, first=1, last=plane, step=1):
         @pl.loop(first, last, step=step)
         def _(d):
@@ -221,26 +226,29 @@
 
     pl.semaphore_wait(bar, plane - 1 + len(STEPS) + 1)
 
-    def template_copy(q, src_of):
-        return remote(tsend.at[tile_of(q)], tbuf.at[tile_of(src_of)], t_s.at[q], t_r.at[src_of], mate(q))
-
-    each(lambda q: template_copy(q, me).start())
-
-    def image_copy(q, src_of):
-        return remote(
-            image_part(q), img_buf.at[pix, slot(src_of)], i_s.at[q], i_r.at[src_of], mate(q)
-        )
-
-    each(lambda q: image_copy(q, me).start(), 1, plane, 2)
-
-    def swap(q, h):
-        return remote(img_buf.at[h, slot(q)], img_buf.at[h, slot(q)], x_s.at[q], x_r.at[q], twin)
-
-    own.wait()
-    swap(me, pix).start()
+    def template_copy(q):
+        return remote(tsend.at[tile_of(q)], tbuf.at[tile_of(me)], t_s, t_r, mate(q))
+
+    each(lambda q: template_copy(q).start())
+    template_copies = joint(
+        tsend.at[pl.ds(0, others * tile)], tbuf.at[pl.ds(0, others * tile)], t_s, t_r
+    )
+
+    def image_copy(q, g):
+        return remote(image_part(q), img_buf.at[pix, slot(me)], i_s.at[g], i_r.at[g], mate(q))
+
+    def image_copies(g):
+        some = img_buf.at[pix, pl.ds(0, plane // 2 - 1 + g)]
+        return joint(some, some, i_s.at[g], i_r.at[g])
+
+    each(lambda q: image_copy(q, 1).start(), 1, plane, 2)
+
+    def swap(g, h):
+        some = img_buf.at[h, pl.ds(lax.rem(me + g, 2) * (plane // 2), plane // 2)]
+        return remote(some, some, x_s.at[g], x_r.at[g], twin)
 
     tbuf[tile_of(me), :] = tsend[tile_of(me), :]
-    each(lambda q: template_copy(q, q).wait_recv())
+    template_copies.wait_recv()
     for k in range(tile_rows):
         tall[POS[0], :, k * side : (k + 1) * side] = tbuf[
             pl.ds(k, plane, stride=tile), :
@@ -254,27 +262,29 @@
     tall[POS[0], :, full:] = pieces.astype(bf16)
 
     def block(src, dst, step):
-        return remote(tall.at[POS[src]], tall.at[POS[dst]], a_s.at[dst], a_r.at[dst], along(step))
-
-    def arrived(dst):
-        block(dst, dst, 0).wait_recv()
+        way = 3 if dst in LATE else BASE.get(dst, 0)
+        return remote(tall.at[POS[src]], tall.at[POS[dst]], a_s, a_r.at[way], along(step))
+
+    def blocks(count, way):
+        return joint(tall.at[pl.ds(0, count)], tall.at[pl.ds(0, count)], a_s, a_r.at[way])
 
     def relay(k):
-        arrived(k)
+        blocks(1, BASE[k]).wait_recv()
         for m in RELAY_MOVES[k]:
             block(*m).start()
 
     for m in OWN_MOVES:
         block(*m).start()
-    each(lambda q: image_copy(q, me).start(), 2, plane, 2)
-
-    def pass_image(q):
-        image_copy(q, q).wait_recv()
-        swap(q, pix).start()
+    each(lambda q: image_copy(q, 0).start(), 2, plane, 2)
 
     def score_copy(h, q, src_of):
         return remote(
-            ssend.at[h, slot(q)], srecv.at[h, slot(src_of)], s_s.at[h, q], s_r.at[h, src_of], mate(q)
+            ssend.at[h, slot(q)], srecv.at[h, slot(src_of)], s_s.at[h], s_r.at[h], mate(q)
+        )
+
+    def score_copies(h):
+        return joint(
+            ssend.at[h, pl.ds(0, others)], srecv.at[h, pl.ds(0, others)], s_s.at[h], s_r.at[h]
         )
 
     group = 4
@@ -297,21 +307,26 @@
 
         each(lambda q: score_copy(h, q, me).start(), 2 - odd, plane, 2)
 
-    each(pass_image, 1, plane, 2)
+    image_copies(1).wait_recv()
+    swap(1, pix).start()
     relay(5)
     relay(11)
-    for k in EARLY:
-        if k not in BASE:
-            arrived(k)
-    each(lambda q: swap(q, 1 - pix).wait_recv(), 1, plane, 2)
+    blocks(len(EARLY) - len(BASE), 0).wait_recv()
+    swap(1, 1 - pix).wait_recv()
     score_part(0, 1)
-    each(pass_image, 2, plane, 2)
-    each(lambda q: swap(q, 1 - pix).wait_recv(), 0, plane, 2)
+    image_copies(0).wait_recv()
+    own.wait()
+    swap(0, pix).start()
+    swap(0, 1 - pix).wait_recv()
     score_part(0, 0)
-    for k in LATE:
-        arrived(k)
+    blocks(len(LATE), 3).wait_recv()
     score_part(1, 1)
     score_part(1, 0)
+    template_copies.wait_send()
+    for g in range(2):
+        image_copies(g).wait_send()
+        swap(g, pix).wait_send()
+    blocks(NZ - 1, 0).wait_send()
     for h in range(2):
         srecv[h, pl.ds(slot(me), 1)] = ssend[h, pl.ds(slot(me), 1)]
 
@@ -327,7 +342,7 @@
             preferred_element_type=f32,
         )
         gain = prec * lax.rsqrt(norm[:1] + 1e-06)
-        each(lambda q: score_copy(h, q, q).wait_recv())
+        score_copies(h).wait_recv()
         lsend[h] = gain * jnp.sum(srecv[h], axis=0)
         logit_copy(h).start()
     own_top = jnp.max(jnp.maximum(lsend[0], lsend[1]), axis=1, keepdims=True)
@@ -341,24 +356,35 @@
         jnp.exp(lrecv[0] - top) + jnp.exp(lrecv[1] - top), axis=1, keepdims=True
     )
 
-    def resp_copy(h, q, src_of):
-        return remote(
-            rall.at[h, slot(src_of)], rall.at[h, slot(src_of)], r_s.at[h, q], r_r.at[h, src_of], mate(q)
-        )
+    def resp_copy(h, q):
+        mine = rall.at[h, slot(me)]
+        return remote(mine, mine, r_s.at[h], r_r.at[h], mate(q))
+
+    def resp_copies(h):
+        some = rall.at[h, pl.ds(0, others)]
+        return joint(some, some, r_s.at[h], r_r.at[h])
 
     for h in (1, 0):
         rall[h, pl.ds(slot(me), 1)] = (weights[h] / totals).astype(bf16)[None]
-        each(lambda q: resp_copy(h, q, me).start())
+        each(lambda q: resp_copy(h, q).start())
     column = top + jnp.log(totals)
     eye = lax.broadcasted_iota(jnp.int32, (nimg, nimg), 0) == lax.broadcasted_iota(
         jnp.int32, (nimg, nimg), 1
     )
     loglik[...] = jnp.sum(jnp.where(eye, column, 0.0), axis=0, keepdims=True)
 
-    def near_copy(k, step):
-        return remote(sums.at[POS[k]], rr.at[k], z_s.at[k], z_r.at[k], along(step))
-
-    near = {dst: -step for src in RELAY for dst, step in RELAY[src]}
+    for h in range(2):
+        score_copies(h).wait_send()
+        logit_copy(h).wait_send()
+
+    near = {dst: (base, -step) for base in RELAY for dst, step in RELAY[base]}
+
+    def near_copy(k):
+        base, step = near[k]
+        return remote(sums.at[POS[k]], rr.at[k], z_s, z_r.at[BASE[base]], along(step))
+
+    def near_copies(count, base):
+        return joint(sums.at[pl.ds(0, count)], rr.at[pl.ds(0, count)], z_s, z_r.at[BASE[base]])
 
     def far_copy(b):
         j = BASE[b]
@@ -366,8 +392,8 @@
 
     def base_sum(b):
         val = own_sums[BASE[b]]
+        near_copies(len(RELAY[b]), b).wait_recv()
         for k, step in RELAY[b]:
-            near_copy(k, near[k]).wait_recv()
             val = val + rr[k].astype(f32)
         return val
 
@@ -376,7 +402,7 @@
         far_copy(b).start()
 
     for h in (1, 0):
-        each(lambda q: resp_copy(h, q, q).wait_recv())
+        resp_copies(h).wait_recv()
         resp = rall[h].reshape(plane * nimg, ntpl).astype(f32).T.astype(bf16)
         for c in range(2):
             res = lax.dot_general(
@@ -394,7 +420,9 @@
                     own_sums[BASE[k], :, c * part : (c + 1) * part] = res[i * plane : (i + 1) * plane]
         for k in (ORDER[half:] if h else (13, 2, 14, 1, 15)):
             if k in near:
-                near_copy(k, near[k]).start()
+                near_copy(k).start()
+    for h in range(2):
+        resp_copies(h).wait_send()
     for b in FAR:
         send_far(b)
     val = base_sum(0)
@@ -404,12 +432,18 @@
     for k in range(tile_rows):
         fsend[pl.ds(k, plane, stride=tile_rows), :] = val[:, k * side : (k + 1) * side]
 
-    def final_copy(q, src_of):
-        return remote(fsend.at[rows_of(q)], fin.at[rows_of(src_of)], f_s.at[q], f_r.at[src_of], mate(q))
-
-    each(lambda q: final_copy(q, me).start())
+    def final_copy(q):
+        return remote(fsend.at[rows_of(q)], fin.at[rows_of(me)], f_s, f_r, mate(q))
+
+    each(lambda q: final_copy(q).start())
+    final_copies = joint(
+        fsend.at[pl.ds(0, others * tile_rows)], fin.at[pl.ds(0, others * tile_rows)], f_s, f_r
+    )
     fin[rows_of(me), :] = fsend[rows_of(me), :]
-    each(lambda q: final_copy(q, q).wait_recv())
+    near_copies(len(near), 0).wait_send()
+    for b in FAR:
+        far_copy(b).wait_send()
+    final_copies.wait_recv()
     whole = fin[...]
     squares = jnp.sum(jnp.sum(whole * whole, axis=0, keepdims=True), axis=1, keepdims=True)
     scaled = whole * lax.rsqrt(squares / (side * side) + 1e-06)
@@ -421,20 +455,7 @@
     half_copy.start()
     out[pl.ds(pix, 1)] = stage[pl.ds(pix, 1)]
 
-    each(lambda q: image_copy(q, me).wait_send())
-    each(lambda q: swap(q, pix).wait_send(), 0, plane)
-    each(lambda q: template_copy(q, me).wait_send())
-    for m in OWN_MOVES + RELAY_MOVES[5] + RELAY_MOVES[11]:
-        block(*m).wait_send()
-    for h in range(2):
-        each(lambda q: score_copy(h, q, me).wait_send())
-        each(lambda q: resp_copy(h, q, me).wait_send())
-        logit_copy(h).wait_send()
-    for k in near:
-        near_copy(k, near[k]).wait_send()
-    for b in FAR:
-        far_copy(b).wait_send()
-    each(lambda q: final_copy(q, me).wait_send())
+    final_copies.wait_send()
     half_copy.wait_recv()
     out[pl.ds(1 - pix, 1)] = orecv[...][None]
     half_copy.wait_send()
@@ -491,26 +512,26 @@
             pltpu.VMEM((2, half_rows, side), f32),
             pltpu.VMEM((half_rows, side), f32),
             pltpu.VMEM((side, side), f32),
-            dma((plane,)),
-            dma((plane,)),
-            dma((plane,)),
-            dma((plane,)),
-            dma((plane,)),
-            dma((plane,)),
-            dma((NZ,)),
-            dma((NZ,)),
-            dma((2, plane)),
-            dma((2, plane)),
-            dma((2,)),
-            dma((2,)),
-            dma((2, plane)),
-            dma((2, plane)),
-            dma((NZ,)),
-            dma((NZ,)),
+            dma((2,)),
+            dma((2,)),
+            dma((2,)),
+            dma((2,)),
+            dma,
+            dma,
+            dma,
+            dma((4,)),
+            dma((2,)),
+            dma((2,)),
+            dma((2,)),
+            dma((2,)),
+            dma((2,)),
+            dma((2,)),
+            dma,
             dma((len(RELAY),)),
             dma((len(RELAY),)),
-            dma((plane,)),
-            dma((plane,)),
+            dma((len(RELAY),)),
+            dma,
+            dma,
             dma,
             dma,
             dma,

time: 87.9 us -> 85.2 us (0.969)
  Pallas kernels: 83.2 us -> 80.6 us
    pallas_call x1, Pallas kernels: 83.2 us -> 80.6 us  [on_device(): pl.pallas_call(functools.partial(em_kernel, side, min(512, natoms)), out_...]
where the time goes in v5:
time: 85.2 us; the launch traced here: 85.1 us
  Pallas kernels  80.6 us (95%)
  local copies, waits for them, and re-layouts  3.73 us (4%)
    pallas_call x1, Pallas kernels, on_device(): pl.pallas_call(functools.partial(em_kernel, side, min(512, natoms)), out_...  80.6 us
    unnamed x21, local copies, waits for them, and re-layouts  3.73 us

profile of v5, /device:TPU:1, one launch (start us, length us, event | category | flops | bytes accessed | tf_op | source)
XLA Modules:
  0.0 85.1 jit_solution(8202757516482723870)
XLA Ops:
  0.6 0.0 copy-start
  0.6 0.0 copy-start.1
  0.7 0.0 copy-start.2
  0.7 0.0 copy-start.4
  0.7 0.0 copy-start.6
  0.7 0.0 copy-start.7
  0.7 0.0 copy-start.8
  0.7 2.0 %copy.14 = bf16[8,8,64,128]{3,1,2,0:T(8,128)(2,1)S(1)} copy(bf16[8,8,64,128]{3,2,1,0:T(8,128)(2,1)} %bitcast.17) | data formatting | bytes 2097152
  2.7 0.0 copy-start.3
  2.7 0.0 copy-start.5
  2.7 0.0 copy-done
  2.7 0.0 copy-done.1
  2.7 0.0 copy-done.2
  2.7 0.0 copy-done.4
  2.7 0.0 copy-done.6
  2.7 0.0 copy-done.7
  2.7 0.0 copy-done.8
  2.8 0.6 copy-done.3
  3.3 0.0 copy-done.5
  3.3 80.6 %shard_map.113 = (f32[2,64,128]{2,1,0:T(8,128)S(1)}, f32[1,64]{1,0:T(1,128)S(1)}) custom-call(s32[2]{0:T(128)S(1)} %copy-done.5, s32[2]{0:T(128)S(1)} %copy-done.6, f32[5]{0:T(128)S(1)} %copy-done.7, f32[5]{0:T(128)S(1)} %copy-done.8, bf16[64,8192]{1,0:T(8,128)(2,1)S(1)} %bitcast.10, f32[3,8,4096]{2,1,0:T(8,128)S(1)} %bitcast.11, s32[1,4096]{1,0:T(1,128)S(1)} %bitcast.12, ...), custom_call_target="tpu_custom_call" | custom-call | tf_op jit(solution)/shard_map/pallas_call | solution.py:487
  83.9 0.6 copy.17
  84.6 0.5 copy.18
Async XLA Ops:
  0.6 2.1 %copy-start = (f32[8,3,4096]{2,0,1:T(8,128)S(1)}, f32[8,3,4096]{2,0,1:T(8,128)}, u32[]{:S(2)}) copy-start(f32[8,3,4096]{2,0,1:T(8,128)} %param.11) | copy-start | bytes 1179652
  0.6 2.1 %copy-start.1 = (s32[4096]{0:T(1024)S(1)}, s32[4096]{0:T(1024)}, u32[]{:S(2)}) copy-start(s32[4096]{0:T(1024)} %param.12) | copy-start | bytes 49156
  0.7 2.1 %copy-start.2 = (f32[256,3]{0,1:T(4,128)S(1)}, f32[256,3]{0,1:T(4,128)}, u32[]{:S(2)}) copy-start(f32[256,3]{0,1:T(4,128)} %param.15) | copy-start | bytes 9220
  0.7 2.1 %copy-start.4 = (f32[256]{0:T(256)S(1)}, f32[256]{0:T(256)}, u32[]{:S(2)}) copy-start(f32[256]{0:T(256)} %param.19) | copy-start | bytes 3076
  0.7 2.1 %copy-start.6 = (s32[2]{0:T(128)S(1)}, s32[2]{0:T(128)}, u32[]{:S(2)}) copy-start(s32[2]{0:T(128)} %view_sm.1) | copy-start | bytes 28
  0.7 2.1 %copy-start.7 = (f32[5]{0:T(128)S(1)}, f32[5]{0:T(128)}, u32[]{:S(2)}) copy-start(f32[5]{0:T(128)} %tamp_sm.1) | copy-start | bytes 64
  0.7 2.1 %copy-start.8 = (f32[5]{0:T(128)S(1)}, f32[5]{0:T(128)}, u32[]{:S(2)}) copy-start(f32[5]{0:T(128)} %twid_sm.1) | copy-start | bytes 64
  2.7 0.7 copy-start.3
  2.7 0.7 copy-start.5

commit v6 on v5

--- a/solution.py
+++ b/solution.py
@@ -287,7 +287,7 @@
             ssend.at[h, pl.ds(0, others)], srecv.at[h, pl.ds(0, others)], s_s.at[h], s_r.at[h]
         )
 
-    group = 4
+    group = 8
 
     def score_part(h, odd):
         base = lax.rem(me + odd, 2) * (plane // 2)
@@ -485,7 +485,7 @@
     dma = pltpu.SemaphoreType.DMA
     natoms = atom_types.shape[0]
     averages, loglik = pl.pallas_call(
-        functools.partial(em_kernel, side, min(512, natoms)),
+        functools.partial(em_kernel, side, min(1024, natoms)),
         out_shape=(
             jax.ShapeDtypeStruct((2, half_rows, side), f32),
             jax.ShapeDtypeStruct((1, nimg), f32),

time: 85.2 us -> 82.8 us (0.972)
  Pallas kernels: 80.6 us -> 78.1 us
    pallas_call x1, Pallas kernels: 80.6 us -> 78.1 us  [on_device(): pl.pallas_call(functools.partial(em_kernel, side, min(1024, natoms)), out...]
where the time goes in v6:
time: 82.8 us; the launch traced here: 82.6 us
  Pallas kernels  78.1 us (94%)
  local copies, waits for them, and re-layouts  3.73 us (5%)
    pallas_call x1, Pallas kernels, on_device(): pl.pallas_call(functools.partial(em_kernel, side, min(1024, natoms)), out...  78.1 us
    unnamed x21, local copies, waits for them, and re-layouts  3.73 us

profile of v6, /device:TPU:1, one launch (start us, length us, event | category | flops | bytes accessed | tf_op | source)
XLA Modules:
  0.0 82.6 jit_solution(1612052628392318757)
XLA Ops:
  0.6 0.0 copy-start
  0.6 0.0 copy-start.1
  0.7 0.0 copy-start.2
  0.7 0.0 copy-start.4
  0.7 0.0 copy-start.6
  0.7 0.0 copy-start.7
  0.7 0.0 copy-start.8
  0.7 2.0 %copy.14 = bf16[8,8,64,128]{3,1,2,0:T(8,128)(2,1)S(1)} copy(bf16[8,8,64,128]{3,2,1,0:T(8,128)(2,1)} %bitcast.17) | data formatting | bytes 2097152
  2.7 0.0 copy-start.3
  2.7 0.0 copy-start.5
  2.7 0.0 copy-done
  2.7 0.0 copy-done.1
  2.7 0.0 copy-done.2
  2.7 0.0 copy-done.4
  2.7 0.0 copy-done.6
  2.7 0.0 copy-done.7
  2.7 0.0 copy-done.8
  2.8 0.6 copy-done.3
  3.3 0.0 copy-done.5
  3.3 78.1 %shard_map.113 = (f32[2,64,128]{2,1,0:T(8,128)S(1)}, f32[1,64]{1,0:T(1,128)S(1)}) custom-call(s32[2]{0:T(128)S(1)} %copy-done.5, s32[2]{0:T(128)S(1)} %copy-done.6, f32[5]{0:T(128)S(1)} %copy-done.7, f32[5]{0:T(128)S(1)} %copy-done.8, bf16[64,8192]{1,0:T(8,128)(2,1)S(1)} %bitcast.10, f32[3,8,4096]{2,1,0:T(8,128)S(1)} %bitcast.11, s32[1,4096]{1,0:T(1,128)S(1)} %bitcast.12, ...), custom_call_target="tpu_custom_call" | custom-call | tf_op jit(solution)/shard_map/pallas_call | solution.py:487
  81.5 0.6 copy.17
  82.1 0.5 copy.18
Async XLA Ops:
  0.6 2.1 %copy-start = (f32[8,3,4096]{2,0,1:T(8,128)S(1)}, f32[8,3,4096]{2,0,1:T(8,128)}, u32[]{:S(2)}) copy-start(f32[8,3,4096]{2,0,1:T(8,128)} %param.11) | copy-start | bytes 1179652
  0.6 2.1 %copy-start.1 = (s32[4096]{0:T(1024)S(1)}, s32[4096]{0:T(1024)}, u32[]{:S(2)}) copy-start(s32[4096]{0:T(1024)} %param.12) | copy-start | bytes 49156
  0.7 2.1 %copy-start.2 = (f32[256,3]{0,1:T(4,128)S(1)}, f32[256,3]{0,1:T(4,128)}, u32[]{:S(2)}) copy-start(f32[256,3]{0,1:T(4,128)} %param.15) | copy-start | bytes 9220
  0.7 2.1 %copy-start.4 = (f32[256]{0:T(256)S(1)}, f32[256]{0:T(256)}, u32[]{:S(2)}) copy-start(f32[256]{0:T(256)} %param.19) | copy-start | bytes 3076
  0.7 2.1 %copy-start.6 = (s32[2]{0:T(128)S(1)}, s32[2]{0:T(128)}, u32[]{:S(2)}) copy-start(s32[2]{0:T(128)} %view_sm.1) | copy-start | bytes 28
  0.7 2.1 %copy-start.7 = (f32[5]{0:T(128)S(1)}, f32[5]{0:T(128)}, u32[]{:S(2)}) copy-start(f32[5]{0:T(128)} %tamp_sm.1) | copy-start | bytes 64
  0.7 2.1 %copy-start.8 = (f32[5]{0:T(128)S(1)}, f32[5]{0:T(128)}, u32[]{:S(2)}) copy-start(f32[5]{0:T(128)} %twid_sm.1) | copy-start | bytes 64
  2.7 0.7 copy-start.3
  2.7 0.7 copy-start.5

commit v7 on v6

--- a/solution.py
+++ b/solution.py
@@ -143,7 +143,7 @@
     others = plane - 1
 
     def each(body, first=1, last=plane, step=1):
-        @pl.loop(first, last, step=step)
+        @pl.loop(first, last, step=step, unroll=True)
         def _(d):
             body(lax.rem(me + d, plane))
 

time: 82.8 us -> 82.8 us (level)
  no operation moved by 1% of the time
where the time goes in v7:
time: 82.8 us; the launch traced here: 82.6 us
  Pallas kernels  78.1 us (94%)
  local copies, waits for them, and re-layouts  3.73 us (5%)
    pallas_call x1, Pallas kernels, on_device(): pl.pallas_call(functools.partial(em_kernel, side, min(1024, natoms)), out...  78.1 us
    unnamed x21, local copies, waits for them, and re-layouts  3.73 us

profile of v7, /device:TPU:1, one launch (start us, length us, event | category | flops | bytes accessed | tf_op | source)
XLA Modules:
  0.0 82.6 jit_solution(1446000002480057740)
XLA Ops:
  0.6 0.0 copy-start
  0.6 0.0 copy-start.1
  0.7 0.0 copy-start.2
  0.7 0.0 copy-start.4
  0.7 0.0 copy-start.6
  0.7 0.0 copy-start.7
  0.7 0.0 copy-start.8
  0.7 2.0 %copy.14 = bf16[8,8,64,128]{3,1,2,0:T(8,128)(2,1)S(1)} copy(bf16[8,8,64,128]{3,2,1,0:T(8,128)(2,1)} %bitcast.17) | data formatting | bytes 2097152
  2.7 0.0 copy-start.3
  2.7 0.0 copy-start.5
  2.7 0.0 copy-done
  2.7 0.0 copy-done.1
  2.7 0.0 copy-done.2
  2.7 0.0 copy-done.4
  2.7 0.0 copy-done.6
  2.7 0.0 copy-done.7
  2.7 0.0 copy-done.8
  2.8 0.6 copy-done.3
  3.3 0.0 copy-done.5
  3.3 78.1 %shard_map.113 = (f32[2,64,128]{2,1,0:T(8,128)S(1)}, f32[1,64]{1,0:T(1,128)S(1)}) custom-call(s32[2]{0:T(128)S(1)} %copy-done.5, s32[2]{0:T(128)S(1)} %copy-done.6, f32[5]{0:T(128)S(1)} %copy-done.7, f32[5]{0:T(128)S(1)} %copy-done.8, bf16[64,8192]{1,0:T(8,128)(2,1)S(1)} %bitcast.10, f32[3,8,4096]{2,1,0:T(8,128)S(1)} %bitcast.11, s32[1,4096]{1,0:T(1,128)S(1)} %bitcast.12, ...), custom_call_target="tpu_custom_call" | custom-call | tf_op jit(solution)/shard_map/pallas_call | solution.py:487
  81.5 0.6 copy.17
  82.1 0.5 copy.18
Async XLA Ops:
  0.6 2.1 %copy-start = (f32[8,3,4096]{2,0,1:T(8,128)S(1)}, f32[8,3,4096]{2,0,1:T(8,128)}, u32[]{:S(2)}) copy-start(f32[8,3,4096]{2,0,1:T(8,128)} %param.11) | copy-start | bytes 1179652
  0.6 2.1 %copy-start.1 = (s32[4096]{0:T(1024)S(1)}, s32[4096]{0:T(1024)}, u32[]{:S(2)}) copy-start(s32[4096]{0:T(1024)} %param.12) | copy-start | bytes 49156
  0.7 2.1 %copy-start.2 = (f32[256,3]{0,1:T(4,128)S(1)}, f32[256,3]{0,1:T(4,128)}, u32[]{:S(2)}) copy-start(f32[256,3]{0,1:T(4,128)} %param.15) | copy-start | bytes 9220
  0.7 2.1 %copy-start.4 = (f32[256]{0:T(256)S(1)}, f32[256]{0:T(256)}, u32[]{:S(2)}) copy-start(f32[256]{0:T(256)} %param.19) | copy-start | bytes 3076
  0.7 2.1 %copy-start.6 = (s32[2]{0:T(128)S(1)}, s32[2]{0:T(128)}, u32[]{:S(2)}) copy-start(s32[2]{0:T(128)} %view_sm.1) | copy-start | bytes 28
  0.7 2.1 %copy-start.7 = (f32[5]{0:T(128)S(1)}, f32[5]{0:T(128)}, u32[]{:S(2)}) copy-start(f32[5]{0:T(128)} %tamp_sm.1) | copy-start | bytes 64
  0.7 2.1 %copy-start.8 = (f32[5]{0:T(128)S(1)}, f32[5]{0:T(128)}, u32[]{:S(2)}) copy-start(f32[5]{0:T(128)} %twid_sm.1) | copy-start | bytes 64
  2.7 0.7 copy-start.3
  2.7 0.7 copy-start.5
